TPU v7x, 128 devices: a whole 4x4x4 slice. The times are simulated.
128 devices in a mesh: fsdp: 16 (over y_hi, x, core), tp: 8 (over y_lo, z).
Axes of the slice: x: 4, y: 4 (y_hi: 2, y_lo: 2; y = y_hi * 2 + y_lo), z: 4, core: 2. Of those that a mesh axis runs over, the one named last changes fastest.
Arguments:
- hidden_in: bfloat16 [8192, 4096], P('fsdp'), may hold values from -6 to 6
- w_gate: bfloat16 [4096, 8192], P(('fsdp', 'tp')), may hold values from -0.09375 to 0.09375
- w_input: bfloat16 [4096, 8192], P(('fsdp', 'tp')), may hold values from -0.09375 to 0.09375
- w_groups: bfloat16 [4096, 4096], P(('fsdp', 'tp')), may hold values from -0.09375 to 0.09375
- w_step: bfloat16 [4096, 128], P(('fsdp', 'tp')), may hold values from -0.09375 to 0.09375
- w_out: bfloat16 [8192, 4096], P('tp', 'fsdp'), may hold values from -0.0625 to 0.0625
- conv_input: bfloat16 [4, 8192], P(None, 'tp'), may hold values from -3 to 3
- conv_groups: bfloat16 [4, 4096], P(None, 'tp'), may hold values from -3 to 3
- tail_input: bfloat16 [64, 3, 8192], P('fsdp', None, 'tp'), may hold values from -6 to 6
- tail_groups: bfloat16 [64, 3, 4096], P('fsdp', None, 'tp'), may hold values from -6 to 6
- init_state: float32 [64, 128, 64, 256], P('fsdp', 'tp'), may hold values from -2.4 to 2.4
- a_rate: float32 [128], P('tp'), as said below
- step_bias: float32 [128], P('tp'), may hold values from -3.5 to -2.5
- skip_gain: float32 [128], P('tp'), may hold values from 0.5 to 1.5
- norm_gain: float32 [8192], P('tp'), may hold values from 0.1 to 1.9
- offsets: int32 [64], P('fsdp'), may hold values from 1 to 128, as said below
Outputs:
- mixed: bfloat16 [8192, 4096], P(('fsdp', 'tp'))
- final_state: float32 [64, 128, 64, 256], P('fsdp', 'tp')
Inputs may be any that keep to these rules, and one draw needn't show every extreme that they name: `a_rate`: rates of the heads' decay; positive. `offsets`: every offset lies in 1 to 128; some rollout has all 128 tokens live in every draw.
All inputs are finite; a program needn't handle non-finite values.
Results may differ from a plain program's by a relative error of at most 0.024.
Values may be sent and summed in bfloat16 or wider, within the bound.
No kernel may reach another device: no remote copies, remote signals or barrier semaphores. Data moves between devices by JAX's collectives and lax.ppermute only.
A program may use at most 128 MiB of HBM per device.

v0:
```python
import functools

import jax
import jax.numpy as jnp
from jax import lax
from jax.experimental import pallas as pl
from jax.experimental.pallas import tpu as pltpu
from jax.sharding import Mesh
from jax.sharding import PartitionSpec as P

P_SIZE = 64
N = 256
CONV = 4
LEN = 128
HEADS = 16
CH = HEADS * P_SIZE
HALF = CH // 2
WIDTH = 2 * N // 2 + CH
KB = 512
FAST = 48 * 1024 * 1024

F32 = jnp.float32
BF16 = jnp.bfloat16
NT = (((1,), (1,)), ((), ()))


def ring(n, step):
    return [(i, (i + step) % n) for i in range(n)]


def swap(value, axis):
    return lax.ppermute(value, axis, [(0, 1), (1, 0)])


def after(value, *others):
    return lax.optimization_barrier((value,) + others)[0]


def right(value, *others):
    return lax.ppermute(after(value, *others), "x", ring(4, 1))


def left(value, *others):
    return lax.ppermute(after(value, *others), "x", ring(4, -1))


def over(value, *others):
    return swap(after(value, *others), "yh")


def assemble_kernel(blocks_ref, out_ref):
    out_ref[:KB, :] = blocks_ref[:, :WIDTH]
    out_ref[KB:, :] = jnp.zeros((16, WIDTH), BF16)
    steps = blocks_ref[:, WIDTH:].astype(F32).T
    out_ref[KB:, :KB] = steps[:16].astype(BF16)


def assemble(blocks):
    return pl.pallas_call(
        assemble_kernel,
        out_shape=jax.ShapeDtypeStruct((KB + 16, WIDTH), BF16),
        compiler_params=pltpu.CompilerParams(vmem_limit_bytes=16 * 1024 * 1024),
        name="assemble",
    )(blocks)


def project_kernel(steps, last, table, own_ref, oth_ref, *refs):
    pieces, refs = refs[:5], refs[5:]
    sums, refs = (refs[:2], refs[2:]) if last else ((None, None), refs)
    out_own, out_oth, weights, turned = refs
    step = pl.program_id(0)
    tiles = pl.num_programs(0) // 2
    half = KB // 2

    @pl.when(step == 0)
    def _():
        for ref, block, skip, rows in zip(pieces, (0, 1, 2, 2, 3), (0, 0, 0, half, 0), (KB, KB, half, half, KB)):
            start = pl.multiple_of(table[1 + block] * KB + skip, half)
            weights[pl.ds(start, rows), :] = ref[:rows, :]
            if steps and ref.shape[0] > rows:
                start = pl.multiple_of(table[1 + block] * KB, KB)
                turned[:, pl.ds(start, KB)] = ref[rows:, :KB]

    def run(hid_ref, sum_ref, out_ref):
        hid = hid_ref[...]
        width = weights.shape[1]
        total = jnp.dot(hid, weights[...], preferred_element_type=F32)
        if last:
            total = total + sum_ref[:, :width]
        out_ref[:, :width] = total.astype(out_ref.dtype)
        if steps:
            extra = lax.dot_general(hid, turned[...], NT, preferred_element_type=F32)
            if last:
                extra = extra + sum_ref[:, width : width + steps]
            out_ref[:, width:] = jnp.zeros((out_ref.shape[0], out_ref.shape[1] - width), out_ref.dtype)
            out_ref[:, width : width + steps] = extra.astype(out_ref.dtype)

    @pl.when(step < tiles)
    def _():
        run(own_ref, sums[0], out_own)

    @pl.when(step >= tiles)
    def _():
        run(oth_ref, sums[1], out_oth)


def project_part(own, oth, pieces, dy, steps=0, sums=()):
    rows, depth = own.shape[0], own.shape[1] // 2
    pieces = [part for piece in pieces for part in (piece if isinstance(piece, tuple) else (piece,))]
    width = pieces[0].shape[1]
    out_width = width + (128 if steps else 0)
    tile = 256
    tiles = rows // tile
    x = lax.axis_index("x")
    yh = (lax.axis_index("yh") + dy) % 2
    table = jnp.stack([yh] + [(x + dx) % 4 for dx in range(4)]).astype(jnp.int32)

    def first(i, _):
        return (jnp.minimum(i, tiles - 1), 0)

    def second(i, _):
        return (jnp.maximum(i - tiles, 0), 0)

    outs = [pl.BlockSpec((tile, out_width), first), pl.BlockSpec((tile, out_width), second)]
    return pl.pallas_call(
        functools.partial(project_kernel, steps, bool(sums)),
        grid_spec=pltpu.PrefetchScalarGridSpec(
            num_scalar_prefetch=1,
            grid=(2 * tiles,),
            in_specs=[
                pl.BlockSpec((tile, depth), lambda i, t: (jnp.minimum(i, tiles - 1), t[0])),
                pl.BlockSpec((tile, depth), lambda i, t: (jnp.maximum(i - tiles, 0), t[0])),
            ]
            + [pl.BlockSpec(p.shape, lambda i, _: (0, 0)) for p in pieces]
            + (outs if sums else []),
            out_specs=outs,
            scratch_shapes=[pltpu.VMEM((depth, width), BF16), pltpu.VMEM((16, depth), BF16)],
        ),
        out_shape=[jax.ShapeDtypeStruct((rows, out_width), BF16 if sums else F32)] * 2,
        compiler_params=pltpu.CompilerParams(vmem_limit_bytes=FAST),
        cost_estimate=pl.CostEstimate(
            flops=4 * rows * depth * width, bytes_accessed=4 * rows * depth + 2 * depth * width, transcendentals=0
        ),
        name="project",
    )(table, own, oth, *pieces, *sums)


def silu(v):
    return v / (1.0 + jnp.exp(-v))


def scan_kernel(
    info, own, got, tail_x, tail_g, conv_x, conv_g, init, rate, bias, skip, gain, out_ref, final_ref, buf_x, buf_g
):
    first = info[0] == 0
    live_to = info[1 + pl.program_id(0)]

    buf_x[8 - (CONV - 1) : 8, :] = tail_x[0].astype(F32)
    buf_g[8 - (CONV - 1) : 8, :] = tail_g[0].astype(F32)
    own_v, got_v = own[...].astype(F32), got[...].astype(F32)
    bo_v, br_v = own_v[:, :N], got_v[:, :N]
    xo_v, xr_v = own_v[:, N : N + HALF], got_v[:, N : N + HALF]
    zo_v, zr_v = own_v[:, N + HALF : WIDTH], got_v[:, N + HALF : WIDTH]
    buf_x[8:, :HALF] = jnp.where(first, xo_v, xr_v)
    buf_x[8:, HALF:] = jnp.where(first, xr_v, xo_v)
    buf_g[8:, :N] = jnp.where(first, bo_v, br_v)
    buf_g[8:, N:] = jnp.where(first, br_v, bo_v)

    def conv(buf, taps_ref):
        taps = taps_ref[...].astype(F32)
        total = None
        for k in range(CONV):
            start = 8 - (CONV - 1) + k
            term = taps[k : k + 1, :] * buf[start : start + LEN, :]
            total = term if total is None else total + term
        return silu(total)

    x = conv(buf_x, conv_x)
    bc = conv(buf_g, conv_g).astype(BF16)
    b, c = bc[:, :N], bc[:, N:]

    rows = lax.broadcasted_iota(jnp.int32, (LEN, LEN), 0)
    cols = lax.broadcasted_iota(jnp.int32, (LEN, LEN), 1)
    raw = own_v[:, WIDTH:] + got_v[:, WIDTH:] + bias[...]
    step = jnp.maximum(raw, 0.0) + jnp.log1p(jnp.exp(-jnp.abs(raw)))
    step = jnp.where((rows < live_to) & (cols < HEADS), step, 0.0)
    lower = (rows >= cols).astype(F32)
    total = jnp.dot(lower, -rate[...] * step, precision=lax.Precision.HIGHEST, preferred_element_type=F32)
    step_t = step.T
    total_t = total.T
    end_t = total_t[:, LEN - 1 : LEN]
    grow_t = jnp.exp(total_t)
    rest_t = jnp.exp(end_t - total_t) * step_t
    end = jnp.exp(end_t)

    scores = lax.dot_general(b, c, NT, preferred_element_type=F32)
    scores = jnp.where(rows <= cols, scores, 0.0)
    x_t = x.T
    init_all = init[...].reshape(CH, N)
    carried = lax.dot_general(init_all.astype(BF16), c, NT, preferred_element_type=F32)
    parts = []
    for h in range(HEADS):
        at = slice(h * P_SIZE, (h + 1) * P_SIZE)
        decay = jnp.exp(jnp.minimum(total_t[h : h + 1, :] - total[:, h : h + 1], 0.0))
        mixing = (decay * scores).astype(BF16)
        weighted = (x_t[at] * step_t[h : h + 1, :]).astype(BF16)
        inner = jnp.dot(weighted, mixing, preferred_element_type=F32)
        parts.append(inner + carried[at] * grow_t[h : h + 1, :])
        kept = (x_t[at] * rest_t[h : h + 1, :]).astype(BF16)
        final_ref[0, h] = init[0, h] * end[h : h + 1, :] + jnp.dot(kept, b, preferred_element_type=F32)
    y = jnp.concatenate(parts, axis=0).T
    y = y + skip[...] * x
    low = y[:, :HALF] * silu(jnp.where(first, zo_v, zr_v))
    high = y[:, HALF:] * silu(jnp.where(first, zr_v, zo_v))
    square = jnp.sum(low * low, axis=-1, keepdims=True) + jnp.sum(high * high, axis=-1, keepdims=True)
    scale = lax.rsqrt(square * (1.0 / CH) + 1e-05)
    low = (low * scale * gain[:, :HALF]).astype(BF16)
    high = (high * scale * gain[:, HALF:]).astype(BF16)
    for side in range(2):
        place = info[5 + 2 * pl.program_id(0) + side]
        at = pl.ds(pl.multiple_of(place * (LEN // 2), LEN // 2), LEN // 2)
        out_ref[at, :HALF] = low[side * LEN // 2 : (side + 1) * LEN // 2]
        out_ref[at, HALF:] = high[side * LEN // 2 : (side + 1) * LEN // 2]


def scan(info, own, got, tail_x, tail_g, conv_x, conv_g, init, rate, bias, skip, gain):
    rollouts = init.shape[0]

    def rows(i, _):
        return (i, 0)

    def whole(i, _):
        return (0, 0)

    return pl.pallas_call(
        scan_kernel,
        grid_spec=pltpu.PrefetchScalarGridSpec(
            num_scalar_prefetch=1,
            grid=(rollouts,),
            in_specs=[
                pl.BlockSpec((LEN, WIDTH + 128), rows),
                pl.BlockSpec((LEN, WIDTH + 128), rows),
                pl.BlockSpec((1, CONV - 1, CH), lambda i, _: (i, 0, 0)),
                pl.BlockSpec((1, CONV - 1, 2 * N), lambda i, _: (i, 0, 0)),
                pl.BlockSpec((CONV, CH), whole),
                pl.BlockSpec((CONV, 2 * N), whole),
                pl.BlockSpec((1, HEADS, P_SIZE, N), lambda i, _: (i, 0, 0, 0)),
                pl.BlockSpec((1, 128), whole),
                pl.BlockSpec((1, 128), whole),
                pl.BlockSpec((1, CH), whole),
                pl.BlockSpec((1, CH), whole),
            ],
            out_specs=[
                pl.BlockSpec((rollouts * LEN, CH), whole),
                pl.BlockSpec((1, HEADS, P_SIZE, N), lambda i, _: (i, 0, 0, 0)),
            ],
            scratch_shapes=[pltpu.VMEM((8 + LEN, CH), F32), pltpu.VMEM((8 + LEN, 2 * N), F32)],
        ),
        out_shape=[
            jax.ShapeDtypeStruct((rollouts * LEN, CH), BF16),
            jax.ShapeDtypeStruct(init.shape, F32),
        ],
        compiler_params=pltpu.CompilerParams(vmem_limit_bytes=FAST),
        cost_estimate=pl.CostEstimate(flops=2_000_000_000, bytes_accessed=14_000_000, transcendentals=4_000_000),
        name="scan",
    )(info, own, got, tail_x, tail_g, conv_x, conv_g, init, rate, bias, skip, gain)


def place_kernel(table, kept_ref, given_ref, out_ref):
    for side, ref in enumerate((kept_ref, given_ref)):
        for index in range(8):
            start = pl.multiple_of(table[8 * side + index] * N, N)
            out_ref[:, pl.ds(start, N)] = ref[:, index * N : (index + 1) * N]


def place(table, kept, given):
    rows, width = kept.shape
    return pl.pallas_call(
        place_kernel,
        grid_spec=pltpu.PrefetchScalarGridSpec(
            num_scalar_prefetch=1,
            grid=(1,),
            in_specs=[pl.BlockSpec((rows, width), lambda i, _: (0, 0))] * 2,
            out_specs=pl.BlockSpec((rows, 2 * width), lambda i, _: (0, 0)),
        ),
        out_shape=jax.ShapeDtypeStruct((rows, 2 * width), BF16),
        compiler_params=pltpu.CompilerParams(vmem_limit_bytes=FAST),
        name="place",
    )(table, kept, given)


def multiply_kernel(split, own_ref, oth_ref, *refs):
    pieces, (first_ref, second_ref, rows) = refs[:-3], refs[-3:]
    per = own_ref.shape[0] // 4
    for dz in range(4):
        for f, ref in enumerate((own_ref, oth_ref)):
            rows[(2 * dz + f) * per : (2 * dz + f + 1) * per, :] = ref[dz * per : (dz + 1) * per, :]
    depth = rows.shape[1]
    for which, out_ref in ((pieces[:split], first_ref), (pieces[split:], second_ref)):
        column = 0
        at = 0
        while at < len(which):
            ref = which[at]
            width = ref.shape[1]
            if ref.shape[0] == depth:
                total = jnp.dot(rows[...], ref[...], preferred_element_type=F32)
                at += 1
            else:
                total = jnp.dot(rows[:, : depth // 2], ref[...], preferred_element_type=F32)
                total += jnp.dot(rows[:, depth // 2 :], which[at + 1][...], preferred_element_type=F32)
                at += 2
            out_ref[:, column : column + width] = total.astype(BF16)
            column += width


def multiply(own, oth, first, second):
    rows, depth = own.shape

    def flat(pieces):
        return [part for piece in pieces for part in (piece if isinstance(piece, tuple) else (piece,))]

    def columns(pieces):
        return sum(p[0].shape[1] if isinstance(p, tuple) else p.shape[1] for p in pieces)

    total = columns(first) + columns(second)
    return pl.pallas_call(
        functools.partial(multiply_kernel, len(flat(first))),
        out_shape=[jax.ShapeDtypeStruct((2 * rows, columns(p)), BF16) for p in (first, second)],
        scratch_shapes=[pltpu.VMEM((2 * rows, depth), BF16)],
        compiler_params=pltpu.CompilerParams(vmem_limit_bytes=36 * 1024 * 1024),
        cost_estimate=pl.CostEstimate(
            flops=4 * rows * depth * total, bytes_accessed=4 * rows * depth + 2 * total * (depth + 2 * rows), transcendentals=0
        ),
        name="multiply",
    )(own, oth, *flat(first), *flat(second))


def add(*terms):
    return functools.reduce(jnp.add, [t.astype(F32) for t in terms]).astype(BF16)


def reduce_z(parts):
    far = parts(2)
    half = far.shape[1] // 2
    far_a = lax.ppermute(far[:, :half], "z", ring(4, 1))
    far_b = lax.ppermute(far[:, half:], "z", ring(4, -1))
    up, down = parts(1), parts(3)
    up = jnp.concatenate([add(up[:, :half], far_a), up[:, half:]], axis=1)
    down = jnp.concatenate([down[:, :half], add(down[:, half:], far_b)], axis=1)
    from_below = lax.ppermute(up, "z", ring(4, 1))
    from_above = lax.ppermute(down, "z", ring(4, -1))
    return add(parts(0), from_below, from_above)


def reduce_z_first(value):
    block = value.shape[0] // 4
    mine = reduce_z(lambda dz: value[dz * block : (dz + 1) * block])
    mine = mine.reshape(2, 2, block // 4, mine.shape[1])
    return add(mine[:, 0], swap(mine[:, 1], "yl"))


def reduce_yl_first(value):
    block = value.shape[0] // 16
    value = value.reshape(8, 2, block, value.shape[1])
    value = add(value[:, 0], swap(value[:, 1], "yl")).reshape(8 * block, value.shape[3])
    mine = reduce_z(lambda dz: value[dz * 2 * block : (dz + 1) * 2 * block])
    return mine.reshape(2, block, mine.shape[1])


def shards(
    hidden_in,
    w_gate,
    w_input,
    w_groups,
    w_step,
    w_out,
    conv_input,
    conv_groups,
    tail_input,
    tail_groups,
    init_state,
    a_rate,
    step_bias,
    skip_gain,
    norm_gain,
    offsets,
):
    yh, x, c = lax.axis_index("yh"), lax.axis_index("x"), lax.axis_index("c")
    yl, z = lax.axis_index("yl"), lax.axis_index("z")
    group = ("c", "yl", "z")
    rows = w_gate.shape[0]

    def by_owner(weight):
        width = weight.shape[1] // 16
        return weight.reshape(rows, 8, 2, width).transpose(2, 1, 0, 3).reshape(16 * rows, width)

    steps = by_owner(w_step).reshape(2, 8 * rows, 8)
    steps = jnp.concatenate([jnp.pad(steps[core], ((0, 0), (8 * core, 120 - 8 * core))) for core in range(2)])
    blocks = jnp.concatenate([by_owner(w_groups), by_owner(w_input), by_owner(w_gate), steps], axis=1)
    s_own = assemble(lax.all_to_all(blocks, group, 0, 0, tiled=True))
    hidden_oth = swap(hidden_in, "c")

    half = KB // 2
    w_r, w_l, w_o = right(w_out), left(w_out), over(w_out)
    s_r, s_l, s_o = right(s_own, w_r, w_l), left(s_own, w_r, w_l), over(s_own, w_o)
    s_ft, s_fb = right(s_r[:half], s_l), left(s_l[half:], s_r)
    near = project_part(hidden_in, hidden_oth, [s_own, s_l, (s_ft, s_fb), s_r], 0, 16)
    s_or, s_ol = right(s_o, s_ft, s_fb), left(s_o, s_ft, s_fb)
    s_oft, s_ofb = over(s_ft), over(s_fb)
    own, oth = project_part(hidden_in, hidden_oth, [s_o, s_ol, (s_oft, s_ofb), s_or], 1, 16, near)
    w_ft, w_fb = right(w_r[:KB], s_or, s_ol), left(w_l[KB:], s_or, s_ol)
    w_or, w_ol = right(w_o, s_or, s_ol), left(w_o, s_or, s_ol)
    w_oft, w_ofb = over(w_ft, s_oft, s_ofb), over(w_fb, s_oft, s_ofb)
    got = swap(after(oth, w_ft, w_fb), "c")

    def lanes(vector):
        return jnp.pad(vector, (0, 128 - HEADS))[None, :]

    at = jnp.arange(8)
    places = ((at % 4 - z) % 4) * 2 + (at // 4 + yl) % 2
    normed, final_state = scan(
        jnp.concatenate([jnp.reshape(c, (1,)), offsets, places]).astype(jnp.int32),
        own,
        got,
        tail_input,
        tail_groups,
        conv_input,
        conv_groups,
        init_state,
        lanes(a_rate),
        lanes(step_bias),
        jnp.repeat(skip_gain, P_SIZE)[None, :],
        norm_gain[None, :],
    )
    normed_oth = swap(after(normed, w_or, w_ol, w_oft, w_ofb), "c")

    first, second = multiply(
        normed, normed_oth, [w_out, w_l, w_r, w_o], [(w_ft, w_fb), w_ol, (w_oft, w_ofb), w_or]
    )
    first, second = reduce_yl_first(first), reduce_z_first(second)
    sums = jnp.concatenate([first, second], axis=2)
    kept = sums[0]
    given = swap(sums[1], "c")

    order = [((yh + dy) % 2) * 4 + (x + dx) % 4 for dy, dx in ((0, 0), (0, 1), (0, 3), (1, 0), (0, 2), (1, 1), (1, 2), (1, 3))]
    mixed = place(jnp.stack([2 * p + core for core in (c, 1 - c) for p in order]).astype(jnp.int32), kept, given)
    return mixed, final_state


def solution(mesh):
    fine = Mesh(mesh.devices.reshape(2, 4, 2, 2, 4), ("yh", "x", "c", "yl", "z"))
    fsdp = ("yh", "x", "c")
    tp = ("yl", "z")
    return jax.shard_map(
        shards,
        mesh=fine,
        in_specs=(
            P(fsdp, None),
            P(fsdp + tp, None),
            P(fsdp + tp, None),
            P(fsdp + tp, None),
            P(fsdp + tp, None),
            P(tp, fsdp),
            P(None, tp),
            P(None, tp),
            P(fsdp, None, tp),
            P(fsdp, None, tp),
            P(fsdp, tp, None, None),
            P(tp),
            P(tp),
            P(tp),
            P(tp),
            P(fsdp),
        ),
        out_specs=(P(fsdp + tp, None), P(fsdp, tp, None, None)),
        check_vma=False,
    )
```

profile of v0, /device:TPU:1, one launch (start us, length us, event | category | flops | bytes accessed | tf_op | source)
XLA Modules:
  0.0 210.8 jit_solution(16289238206563974228)
XLA Ops:
  5.8 7.8 %all-to-all-start = ((bf16[16,32,1408]{2,1,0:T(8,128)(2,1)}), bf16[16,32,1408]{2,1,0:T(8,128)(2,1)S(1)}, u32[]{:S(2)}, u32[]{:S(2)}) async-start(bf16[16,32,1408]{2,1,0:T(8,128)(2,1)} %pad_maximum_fusion), calls=%async_computation | async-start | bytes 2883584 | tf_op jit(solution)/shard_map/all_to_all | solution.py:400
  16.5 17.7 %all-to-all-done = bf16[16,32,1408]{2,1,0:T(8,128)(2,1)S(1)} async-done(((bf16[16,32,1408]{2,1,0:T(8,128)(2,1)}), bf16[16,32,1408]{2,1,0:T(8,128)(2,1)S(1)}, u32[]{:S(2)}, u32[]{:S(2)}) %all-to-all-start) | async-done | bytes 1441824 | tf_op jit(solution)/shard_map/all_to_all | solution.py:400
  36.9 2.6 %collective-permute-start.1 = (bf16[1024,256]{1,0:T(8,128)(2,1)}, bf16[1024,256]{1,0:T(8,128)(2,1)}, u32[]{:S(2)}, u32[]{:S(2)}) collective-permute-start(bf16[1024,256]{1,0:T(8,128)(2,1)} %refs_0_.1), channel_id=1, source_target_pairs={{0,64},{64,0},{1,65},{65,1},{2,66},{66,2},{3,67},{67,3},{4,68},{68... | collective-permute-start | bytes 1572872 | tf_op jit(solution)/shard_map/ppermute | solution.py:32
  39.5 12.2 %collective-permute-done.1.refs_3_ = bf16[1024,256]{1,0:T(8,128)(2,1)} collective-permute-done((bf16[1024,256]{1,0:T(8,128)(2,1)}, bf16[1024,256]{1,0:T(8,128)(2,1)}, u32[]{:S(2)}, u32[]{:S(2)}) %collective-permute-start.1) | collective-permute-done | bytes 524320 | tf_op jit(solution)/shard_map/ppermute | solution.py:32
  54.3 11.4 %collective-permute-done.6.refs_1_ = bf16[528,1280]{1,0:T(8,128)(2,1)S(1)} collective-permute-done((bf16[528,1280]{1,0:T(8,128)(2,1)S(1)}, bf16[528,1280]{1,0:T(8,128)(2,1)S(1)}, u32[]{:S(2)}, u32[]{:S(2)}) %collective-permute-start.6) | collective-permute-done | bytes 1351712 | tf_op jit(solution)/shard_map/ppermute | solution.py:44
  65.8 3.1 %collective-permute-done.5.refs_4_ = bf16[528,1280]{1,0:T(8,128)(2,1)S(1)} collective-permute-done((bf16[528,1280]{1,0:T(8,128)(2,1)S(1)}, bf16[528,1280]{1,0:T(8,128)(2,1)S(1)}, u32[]{:S(2)}, u32[]{:S(2)}) %collective-permute-start.5) | collective-permute-done | bytes 1351712 | tf_op jit(solution)/shard_map/ppermute | solution.py:40
  71.5 11.6 %collective-permute-done.2.refs_0_ = bf16[528,1280]{1,0:T(8,128)(2,1)} collective-permute-done((bf16[528,1280]{1,0:T(8,128)(2,1)S(1)}, bf16[528,1280]{1,0:T(8,128)(2,1)}, u32[]{:S(2)}, u32[]{:S(2)}) %collective-permute-start.2) | collective-permute-done | bytes 1351712 | tf_op jit(solution)/shard_map/ppermute | solution.py:32
  83.1 3.7 %collective-permute-done.7.refs_2_ = bf16[256,1280]{1,0:T(8,128)(2,1)} collective-permute-done((bf16[256,1280]{1,0:T(8,128)(2,1)S(1)}, bf16[256,1280]{1,0:T(8,128)(2,1)}, u32[]{:S(2)}, u32[]{:S(2)}) %collective-permute-start.7) | collective-permute-done | bytes 655392 | tf_op jit(solution)/shard_map/ppermute | solution.py:40
  86.8 2.7 %collective-permute-start.9 = (bf16[528,1280]{1,0:T(8,128)(2,1)}, bf16[528,1280]{1,0:T(8,128)(2,1)}, u32[]{:S(2)}, u32[]{:S(2)}) collective-permute-start(bf16[528,1280]{1,0:T(8,128)(2,1)} %collective-permute-done.2.refs_0_), channel_id=1, source_target_pairs={{0,48},{16,0},{32,16},{48,32},{1,49},{17,1},{33,17},{49,33},{2,50}... | collective-permute-start | bytes 4055048 | tf_op jit(solution)/shard_map/ppermute | solution.py:44
  95.0 11.8 %project.2 = (f32[512,1408]{1,0:T(8,128)}, f32[512,1408]{1,0:T(8,128)}) custom-call(s32[5]{0:T(128)S(1)} %stack.103.table, bf16[512,4096]{1,0:T(8,128)(2,1)} %own_ref.3, bf16[512,4096]{1,0:T(8,128)(2,1)} %collective-permute-done.oth_ref, bf16[528,1280]{1,0:T(8,128)(2,1)S(1)} %assemble.1.refs_0_, bf16[528,1280]{1,0:T(8,128)(2,1)S(1)} %collective-permute-done.6.refs_1_, ...), custom_call_target="tpu_custom_call" | custom-call | flops 5368709120 | bytes 9437184 | tf_op jit(solution)/shard_map/project/pallas_call | solution.py:125
  106.8 10.6 %collective-permute-done.12.refs_4_ = bf16[528,1280]{1,0:T(8,128)(2,1)} collective-permute-done((bf16[528,1280]{1,0:T(8,128)(2,1)}, bf16[528,1280]{1,0:T(8,128)(2,1)}, u32[]{:S(2)}, u32[]{:S(2)}) %collective-permute-start.12) | collective-permute-done | bytes 1351712 | tf_op jit(solution)/shard_map/ppermute | solution.py:40
  119.9 13.6 %project.3 = (bf16[512,1408]{1,0:T(8,128)(2,1)}, bf16[512,1408]{1,0:T(8,128)(2,1)}) custom-call(s32[5]{0:T(128)S(1)} %stack.101.table, bf16[512,4096]{1,0:T(8,128)(2,1)} %own_ref.3, bf16[512,4096]{1,0:T(8,128)(2,1)} %collective-permute-done.oth_ref, bf16[528,1280]{1,0:T(8,128)(2,1)} %collective-permute-done.2.refs_0_, ...), custom_call_target="tpu_custom_call" | custom-call | flops 5368709120 | bytes 9437184 | tf_op jit(solution)/shard_map/project/pallas_call | solution.py:125
  133.5 3.7 %collective-permute-start.15 = (bf16[512,1408]{1,0:T(8,128)(2,1)}, bf16[512,1408]{1,0:T(8,128)(2,1)S(1)}, u32[]{:S(2)}, u32[]{:S(2)}) collective-permute-start(bf16[512,1408]{1,0:T(8,128)(2,1)} %get-tuple-element.33), channel_id=1, source_target_pairs={{0,8},{8,0},{1,9},{9,1},{2,10},{10,2},{3,11},{11,3},{4,12},{12,4},... | collective-permute-start | bytes 4325384 | tf_op jit(solution)/shard_map/ppermute | solution.py:32
  137.4 3.0 %collective-permute-start.17 = (bf16[1024,256]{1,0:T(8,128)(2,1)}, bf16[1024,256]{1,0:T(8,128)(2,1)S(1)}, u32[]{:S(2)}, u32[]{:S(2)}) collective-permute-start(bf16[1024,256]{1,0:T(8,128)(2,1)} %collective-permute-done.1.refs_3_), channel_id=1, source_target_pairs={{0,48},{16,0},{32,16},{48,32},{1,49},{17,1},{33,17},{49,33},{2,50}... | collective-permute-start | bytes 1572872 | tf_op jit(solution)/shard_map/ppermute | solution.py:44
  145.0 10.4 %scan.1 = (bf16[512,1024]{1,0:T(8,128)(2,1)S(1)}, f32[4,16,64,256]{3,2,1,0:T(8,128)}) custom-call(s32[13]{0:T(128)S(1)} %pad_add_fusion.info, bf16[512,1408]{1,0:T(8,128)(2,1)S(1)} %copy-done.5, bf16[512,1408]{1,0:T(8,128)(2,1)S(1)} %collective-permute-done.15.got, bf16[4,3,1024]{2,1,0:T(4,128)(2,1)S(1)} %copy.43.tail_x, ...), custom_call_target="tpu_custom_call" | custom-call | flops 2000000000 | bytes 14000000 | tf_op jit(solution)/shard_map/scan/pallas_call | solution.py:235
  158.9 6.0 %multiply.1 = (bf16[1024,1024]{1,0:T(8,128)(2,1)S(1)}, bf16[1024,1024]{1,0:T(8,128)(2,1)S(1)}) custom-call(bf16[512,1024]{1,0:T(8,128)(2,1)S(1)} %get-tuple-element.38.own_ref, bf16[512,1024]{1,0:T(8,128)(2,1)S(1)} %collective-permute-done.20.oth_ref, bf16[1024,256]{1,0:T(8,128)(2,1)} %refs_0_.1, bf16[1024,256]{1,0:T(8,128)(2,1)} %collective-permute-done.4.refs_1_, ...), custom_call_target="tpu_custom_call" | custom-call | flops 4294967296 | bytes 10485760 | tf_op jit(solution)/shard_map/multiply/pallas_call | solution.py:326
  167.9 5.8 %collective-permute-done.26 = bf16[256,512]{1,0:T(8,128)(2,1)S(1)} collective-permute-done((bf16[256,512]{1,0:T(8,128)(2,1)S(1)}, bf16[256,512]{1,0:T(8,128)(2,1)S(1)}, u32[]{:S(2)}, u32[]{:S(2)}) %collective-permute-start.26) | collective-permute-done | bytes 262176 | tf_op jit(solution)/shard_map/ppermute | solution.py:345
  174.1 3.0 %collective-permute-start.29 = (bf16[256,1024]{1,0:T(8,128)(2,1)S(1)}, bf16[256,1024]{1,0:T(8,128)(2,1)S(1)}, u32[]{:S(2)}, u32[]{:S(2)}) collective-permute-start(bf16[256,1024]{1,0:T(8,128)(2,1)S(1)} %pad_maximum_fusion.2), channel_id=1, source_target_pairs={{0,3},{1,0},{2,1},{3,2},{4,7},{5,4},{6,5},{7,6},{8,11},{9,8},{10,9... | collective-permute-start | bytes 1572872 | tf_op jit(solution)/shard_map/ppermute | solution.py:351
  177.1 10.4 %collective-permute-done.27 = bf16[256,1024]{1,0:T(8,128)(2,1)S(1)} collective-permute-done((bf16[256,1024]{1,0:T(8,128)(2,1)S(1)}, bf16[256,1024]{1,0:T(8,128)(2,1)S(1)}, u32[]{:S(2)}, u32[]{:S(2)}) %collective-permute-start.27) | collective-permute-done | bytes 524320 | tf_op jit(solution)/shard_map/ppermute | solution.py:350
  187.8 3.9 %collective-permute-done.21 = bf16[8,64,1024]{2,1,0:T(8,128)(2,1)S(1)} collective-permute-done((bf16[8,64,1024]{2,1,0:T(8,128)(2,1)S(1)}, bf16[8,64,1024]{2,1,0:T(8,128)(2,1)S(1)}, u32[]{:S(2)}, u32[]{:S(2)}) %collective-permute-start.21) | collective-permute-done | bytes 1048608 | tf_op jit(solution)/shard_map/ppermute | solution.py:32
  192.7 2.7 %collective-permute-start.24 = (bf16[128,512]{1,0:T(8,128)(2,1)S(1)}, bf16[128,512]{1,0:T(8,128)(2,1)S(1)}, u32[]{:S(2)}, u32[]{:S(2)}) collective-permute-start(bf16[128,512]{1,0:T(8,128)(2,1)S(1)} %get-tuple-element.55), channel_id=1, source_target_pairs={{0,3},{1,0},{2,1},{3,2},{4,7},{5,4},{6,5},{7,6},{8,11},{9,8},{10,9... | collective-permute-start | bytes 393224 | tf_op jit(solution)/shard_map/ppermute | solution.py:346
  197.5 3.1 %collective-permute-start.25 = (bf16[128,1024]{1,0:T(8,128)(2,1)S(1)}, bf16[128,1024]{1,0:T(8,128)(2,1)S(1)}, u32[]{:S(2)}, u32[]{:S(2)}) collective-permute-start(bf16[128,1024]{1,0:T(8,128)(2,1)S(1)} %pad_maximum_fusion.5), channel_id=1, source_target_pairs={{0,3},{1,0},{2,1},{3,2},{4,7},{5,4},{6,5},{7,6},{8,11},{9,8},{10,9... | collective-permute-start | bytes 786440 | tf_op jit(solution)/shard_map/ppermute | solution.py:351
  200.7 3.2 %collective-permute-done.23 = bf16[128,1024]{1,0:T(8,128)(2,1)S(1)} collective-permute-done((bf16[128,1024]{1,0:T(8,128)(2,1)S(1)}, bf16[128,1024]{1,0:T(8,128)(2,1)S(1)}, u32[]{:S(2)}, u32[]{:S(2)}) %collective-permute-start.23) | collective-permute-done | bytes 262176 | tf_op jit(solution)/shard_map/ppermute | solution.py:350
  204.1 4.2 %collective-permute-start.31 = (bf16[64,2048]{1,0:T(8,128)(2,1)S(1)}, bf16[64,2048]{1,0:T(8,128)(2,1)S(1)}, u32[]{:S(2)}, u32[]{:S(2)}) collective-permute-start(bf16[64,2048]{1,0:T(8,128)(2,1)S(1)} %get-tuple-element.52), channel_id=1, source_target_pairs={{0,8},{8,0},{1,9},{9,1},{2,10},{10,2},{3,11},{11,3},{4,12},{12,4},... | collective-permute-start | bytes 786440 | tf_op jit(solution)/shard_map/ppermute | solution.py:32
  (124 shorter events, 41.5 us)
Async XLA Ops:
  5.8 28.4 %all-to-all-start = ((bf16[16,32,1408]{2,1,0:T(8,128)(2,1)}), bf16[16,32,1408]{2,1,0:T(8,128)(2,1)S(1)}, u32[]{:S(2)}, u32[]{:S(2)}) async-start(bf16[16,32,1408]{2,1,0:T(8,128)(2,1)} %pad_maximum_fusion), calls=%async_computation | async-start | bytes 2883584 | tf_op jit(solution)/shard_map/all_to_all | solution.py:400
  13.7 80.0 %collective-permute-start = (bf16[512,4096]{1,0:T(8,128)(2,1)}, bf16[512,4096]{1,0:T(8,128)(2,1)}, u32[]{:S(2)}, u32[]{:S(2)}) collective-permute-start(bf16[512,4096]{1,0:T(8,128)(2,1)} %own_ref.3), channel_id=1, source_target_pairs={{0,8},{8,0},{1,9},{9,1},{2,10},{10,2},{3,11},{11,3},{4,12},{12,4},... | collective-permute-start | bytes 12582920 | tf_op jit(solution)/shard_map/ppermute | solution.py:32
  13.9 20.4 %collective-permute-start.3 = (bf16[1024,256]{1,0:T(8,128)(2,1)}, bf16[1024,256]{1,0:T(8,128)(2,1)S(1)}, u32[]{:S(2)}, u32[]{:S(2)}) collective-permute-start(bf16[1024,256]{1,0:T(8,128)(2,1)} %refs_0_.1), channel_id=1, source_target_pairs={{0,16},{16,32},{32,48},{48,0},{1,17},{17,33},{33,49},{49,1},{2,18}... | collective-permute-start | bytes 1572872 | tf_op jit(solution)/shard_map/ppermute | solution.py:40
  15.1 19.2 %collective-permute-start.4 = (bf16[1024,256]{1,0:T(8,128)(2,1)}, bf16[1024,256]{1,0:T(8,128)(2,1)}, u32[]{:S(2)}, u32[]{:S(2)}) collective-permute-start(bf16[1024,256]{1,0:T(8,128)(2,1)} %refs_0_.1), channel_id=1, source_target_pairs={{0,48},{16,0},{32,16},{48,32},{1,49},{17,1},{33,17},{49,33},{2,50}... | collective-permute-start | bytes 1572872 | tf_op jit(solution)/shard_map/ppermute | solution.py:44
  34.3 31.4 %collective-permute-start.6 = (bf16[528,1280]{1,0:T(8,128)(2,1)S(1)}, bf16[528,1280]{1,0:T(8,128)(2,1)S(1)}, u32[]{:S(2)}, u32[]{:S(2)}) collective-permute-start(bf16[528,1280]{1,0:T(8,128)(2,1)S(1)} %assemble.1.refs_0_), channel_id=1, source_target_pairs={{0,48},{16,0},{32,16},{48,32},{1,49},{17,1},{33,17},{49,33},{2,50}... | collective-permute-start | bytes 4055048 | tf_op jit(solution)/shard_map/ppermute | solution.py:44
  36.9 32.0 %collective-permute-start.5 = (bf16[528,1280]{1,0:T(8,128)(2,1)S(1)}, bf16[528,1280]{1,0:T(8,128)(2,1)S(1)}, u32[]{:S(2)}, u32[]{:S(2)}) collective-permute-start(bf16[528,1280]{1,0:T(8,128)(2,1)S(1)} %assemble.1.refs_0_), channel_id=1, source_target_pairs={{0,16},{16,32},{32,48},{48,0},{1,17},{17,33},{33,49},{49,1},{2,18}... | collective-permute-start | bytes 4055048 | tf_op jit(solution)/shard_map/ppermute | solution.py:40
  36.9 14.8 %collective-permute-start.1 = (bf16[1024,256]{1,0:T(8,128)(2,1)}, bf16[1024,256]{1,0:T(8,128)(2,1)}, u32[]{:S(2)}, u32[]{:S(2)}) collective-permute-start(bf16[1024,256]{1,0:T(8,128)(2,1)} %refs_0_.1), channel_id=1, source_target_pairs={{0,64},{64,0},{1,65},{65,1},{2,66},{66,2},{3,67},{67,3},{4,68},{68... | collective-permute-start | bytes 1572872 | tf_op jit(solution)/shard_map/ppermute | solution.py:32
  51.7 31.4 %collective-permute-start.2 = (bf16[528,1280]{1,0:T(8,128)(2,1)S(1)}, bf16[528,1280]{1,0:T(8,128)(2,1)}, u32[]{:S(2)}, u32[]{:S(2)}) collective-permute-start(bf16[528,1280]{1,0:T(8,128)(2,1)S(1)} %assemble.1.refs_0_), channel_id=1, source_target_pairs={{0,64},{64,0},{1,65},{65,1},{2,66},{66,2},{3,67},{67,3},{4,68},{68... | collective-permute-start | bytes 4055048 | tf_op jit(solution)/shard_map/ppermute | solution.py:32
  68.9 17.9 %collective-permute-start.8 = (bf16[272,1280]{1,0:T(8,128)(2,1)S(1)}, bf16[272,1280]{1,0:T(8,128)(2,1)}, u32[]{:S(2)}, u32[]{:S(2)}) collective-permute-start(bf16[272,1280]{1,0:T(8,128)(2,1)S(1)} %slice.143), channel_id=1, source_target_pairs={{0,48},{16,0},{32,16},{48,32},{1,49},{17,1},{33,17},{49,33},{2,50}... | collective-permute-start | bytes 2088968 | tf_op jit(solution)/shard_map/ppermute | solution.py:44
  70.5 16.3 %collective-permute-start.7 = (bf16[256,1280]{1,0:T(8,128)(2,1)S(1)}, bf16[256,1280]{1,0:T(8,128)(2,1)}, u32[]{:S(2)}, u32[]{:S(2)}) collective-permute-start(bf16[256,1280]{1,0:T(8,128)(2,1)S(1)} %slice.142), channel_id=1, source_target_pairs={{0,16},{16,32},{32,48},{48,0},{1,17},{17,33},{33,49},{49,1},{2,18}... | collective-permute-start | bytes 1966088 | tf_op jit(solution)/shard_map/ppermute | solution.py:40
  86.8 30.6 %collective-permute-start.12 = (bf16[528,1280]{1,0:T(8,128)(2,1)}, bf16[528,1280]{1,0:T(8,128)(2,1)}, u32[]{:S(2)}, u32[]{:S(2)}) collective-permute-start(bf16[528,1280]{1,0:T(8,128)(2,1)} %collective-permute-done.2.refs_0_), channel_id=1, source_target_pairs={{0,16},{16,32},{32,48},{48,0},{1,17},{17,33},{33,49},{49,1},{2,18}... | collective-permute-start | bytes 4055048 | tf_op jit(solution)/shard_map/ppermute | solution.py:40
  86.8 30.6 %collective-permute-start.9 = (bf16[528,1280]{1,0:T(8,128)(2,1)}, bf16[528,1280]{1,0:T(8,128)(2,1)}, u32[]{:S(2)}, u32[]{:S(2)}) collective-permute-start(bf16[528,1280]{1,0:T(8,128)(2,1)} %collective-permute-done.2.refs_0_), channel_id=1, source_target_pairs={{0,48},{16,0},{32,16},{48,32},{1,49},{17,1},{33,17},{49,33},{2,50}... | collective-permute-start | bytes 4055048 | tf_op jit(solution)/shard_map/ppermute | solution.py:44
  89.5 30.3 %collective-permute-start.11 = (bf16[272,1280]{1,0:T(8,128)(2,1)}, bf16[272,1280]{1,0:T(8,128)(2,1)}, u32[]{:S(2)}, u32[]{:S(2)}) collective-permute-start(bf16[272,1280]{1,0:T(8,128)(2,1)} %collective-permute-done.8.refs_3_), channel_id=1, source_target_pairs={{0,64},{64,0},{1,65},{65,1},{2,66},{66,2},{3,67},{67,3},{4,68},{68... | collective-permute-start | bytes 2088968 | tf_op jit(solution)/shard_map/ppermute | solution.py:32
  91.9 27.9 %collective-permute-start.10 = (bf16[256,1280]{1,0:T(8,128)(2,1)}, bf16[256,1280]{1,0:T(8,128)(2,1)}, u32[]{:S(2)}, u32[]{:S(2)}) collective-permute-start(bf16[256,1280]{1,0:T(8,128)(2,1)} %collective-permute-done.7.refs_2_), channel_id=1, source_target_pairs={{0,64},{64,0},{1,65},{65,1},{2,66},{66,2},{3,67},{67,3},{4,68},{68... | collective-permute-start | bytes 1966088 | tf_op jit(solution)/shard_map/ppermute | solution.py:32
  117.4 16.1 %collective-permute-start.14 = (bf16[512,256]{1,0:T(8,128)(2,1)S(1)}, bf16[512,256]{1,0:T(8,128)(2,1)}, u32[]{:S(2)}, u32[]{:S(2)}) collective-permute-start(bf16[512,256]{1,0:T(8,128)(2,1)S(1)} %slice.145), channel_id=1, source_target_pairs={{0,48},{16,0},{32,16},{48,32},{1,49},{17,1},{33,17},{49,33},{2,50}... | collective-permute-start | bytes 786440 | tf_op jit(solution)/shard_map/ppermute | solution.py:44
  119.8 13.7 %collective-permute-start.13 = (bf16[512,256]{1,0:T(8,128)(2,1)S(1)}, bf16[512,256]{1,0:T(8,128)(2,1)}, u32[]{:S(2)}, u32[]{:S(2)}) collective-permute-start(bf16[512,256]{1,0:T(8,128)(2,1)S(1)} %slice.144), channel_id=1, source_target_pairs={{0,16},{16,32},{32,48},{48,0},{1,17},{17,33},{33,49},{49,1},{2,18}... | collective-permute-start | bytes 786440 | tf_op jit(solution)/shard_map/ppermute | solution.py:40
  133.5 10.1 %collective-permute-start.15 = (bf16[512,1408]{1,0:T(8,128)(2,1)}, bf16[512,1408]{1,0:T(8,128)(2,1)S(1)}, u32[]{:S(2)}, u32[]{:S(2)}) collective-permute-start(bf16[512,1408]{1,0:T(8,128)(2,1)} %get-tuple-element.33), channel_id=1, source_target_pairs={{0,8},{8,0},{1,9},{9,1},{2,10},{10,2},{3,11},{11,3},{4,12},{12,4},... | collective-permute-start | bytes 4325384 | tf_op jit(solution)/shard_map/ppermute | solution.py:32
  137.4 18.0 %collective-permute-start.16 = (bf16[1024,256]{1,0:T(8,128)(2,1)}, bf16[1024,256]{1,0:T(8,128)(2,1)S(1)}, u32[]{:S(2)}, u32[]{:S(2)}) collective-permute-start(bf16[1024,256]{1,0:T(8,128)(2,1)} %collective-permute-done.1.refs_3_), channel_id=1, source_target_pairs={{0,16},{16,32},{32,48},{48,0},{1,17},{17,33},{33,49},{49,1},{2,18}... | collective-permute-start | bytes 1572872 | tf_op jit(solution)/shard_map/ppermute | solution.py:40
  137.4 18.0 %collective-permute-start.17 = (bf16[1024,256]{1,0:T(8,128)(2,1)}, bf16[1024,256]{1,0:T(8,128)(2,1)S(1)}, u32[]{:S(2)}, u32[]{:S(2)}) collective-permute-start(bf16[1024,256]{1,0:T(8,128)(2,1)} %collective-permute-done.1.refs_3_), channel_id=1, source_target_pairs={{0,48},{16,0},{32,16},{48,32},{1,49},{17,1},{33,17},{49,33},{2,50}... | collective-permute-start | bytes 1572872 | tf_op jit(solution)/shard_map/ppermute | solution.py:44
  140.5 14.9 %collective-permute-start.19 = (bf16[512,256]{1,0:T(8,128)(2,1)}, bf16[512,256]{1,0:T(8,128)(2,1)S(1)}, u32[]{:S(2)}, u32[]{:S(2)}) collective-permute-start(bf16[512,256]{1,0:T(8,128)(2,1)} %collective-permute-done.14.refs_5_), channel_id=1, source_target_pairs={{0,64},{64,0},{1,65},{65,1},{2,66},{66,2},{3,67},{67,3},{4,68},{68... | collective-permute-start | bytes 786440 | tf_op jit(solution)/shard_map/ppermute | solution.py:32
  143.0 12.5 %collective-permute-start.18 = (bf16[512,256]{1,0:T(8,128)(2,1)}, bf16[512,256]{1,0:T(8,128)(2,1)S(1)}, u32[]{:S(2)}, u32[]{:S(2)}) collective-permute-start(bf16[512,256]{1,0:T(8,128)(2,1)} %collective-permute-done.13.refs_4_), channel_id=1, source_target_pairs={{0,64},{64,0},{1,65},{65,1},{2,66},{66,2},{3,67},{67,3},{4,68},{68... | collective-permute-start | bytes 786440 | tf_op jit(solution)/shard_map/ppermute | solution.py:32
  167.8 23.8 %collective-permute-start.21 = (bf16[8,64,1024]{2,1,0:T(8,128)(2,1)S(1)}, bf16[8,64,1024]{2,1,0:T(8,128)(2,1)S(1)}, u32[]{:S(2)}, u32[]{:S(2)}) collective-permute-start(bf16[8,64,1024]{2,1,0:T(8,128)(2,1)S(1)} %slice_bitcast_fusion), channel_id=1, source_target_pairs={{0,4},{4,0},{1,5},{5,1},{2,6},{6,2},{3,7},{7,3},{8,12},{12,8},{9,1... | collective-permute-start | bytes 3145736 | tf_op jit(solution)/shard_map/ppermute | solution.py:32
  174.0 13.5 %collective-permute-start.27 = (bf16[256,1024]{1,0:T(8,128)(2,1)S(1)}, bf16[256,1024]{1,0:T(8,128)(2,1)S(1)}, u32[]{:S(2)}, u32[]{:S(2)}) collective-permute-start(bf16[256,1024]{1,0:T(8,128)(2,1)S(1)} %pad_maximum_fusion.1), channel_id=1, source_target_pairs={{0,1},{1,2},{2,3},{3,0},{4,5},{5,6},{6,7},{7,4},{8,9},{9,10},{10,1... | collective-permute-start | bytes 1572872 | tf_op jit(solution)/shard_map/ppermute | solution.py:350
  174.1 13.3 %collective-permute-start.29 = (bf16[256,1024]{1,0:T(8,128)(2,1)S(1)}, bf16[256,1024]{1,0:T(8,128)(2,1)S(1)}, u32[]{:S(2)}, u32[]{:S(2)}) collective-permute-start(bf16[256,1024]{1,0:T(8,128)(2,1)S(1)} %pad_maximum_fusion.2), channel_id=1, source_target_pairs={{0,3},{1,0},{2,1},{3,2},{4,7},{5,4},{6,5},{7,6},{8,11},{9,8},{10,9... | collective-permute-start | bytes 1572872 | tf_op jit(solution)/shard_map/ppermute | solution.py:351
  (23 other events, 254.6 us)
where the time goes:
time: 211 us
  waiting for transfers between devices  99 us (47%)
  starting transfers between devices  55.3 us (26%)
  Pallas kernels  43.3 us (21%)
  local copies, waits for them, and re-layouts  9.56 us (5%)
  other arithmetic  2.58 us (1%)
    ppermute x12, waiting for transfers between devices, swap(): return lax.ppermute(value, axis, [(0, 1), (1, 0)])  31.1 us
    pallas_call x2, Pallas kernels, project_part(): pl.pallas_call(functools.partial(project_kernel, steps, bool(sums)), grid...  25.4 us
    ppermute x12, starting transfers between devices, swap(): return lax.ppermute(value, axis, [(0, 1), (1, 0)])  20.9 us
    all_to_all x1, waiting for transfers between devices, shards(): s_own = assemble(lax.all_to_all(blocks, group, 0, 0, tiled=True))  17.7 us
    ppermute x6, waiting for transfers between devices, right(): return lax.ppermute(after(value, *others), 'x', ring(4, 1))  17.5 us
    ppermute x2, waiting for transfers between devices, reduce_z(): from_below = lax.ppermute(up, 'z', ring(4, 1))  13.6 us
    ppermute x6, starting transfers between devices, left(): return lax.ppermute(after(value, *others), 'x', ring(4, -1))  12.5 us
    ppermute x6, waiting for transfers between devices, left(): return lax.ppermute(after(value, *others), 'x', ring(4, -1))  11.4 us
  transfers between devices with their start and end apart: 33, of which 16 were waited for; matrix products, arithmetic and copies ran while one was open for 1% of the time, Pallas kernels for 17%

commit v1 on v0

--- a/solution.py
+++ b/solution.py
@@ -48,6 +48,33 @@
     return swap(after(value, *others), "yh")
 
 
+def deal_kernel(groups_ref, input_ref, gate_ref, step_ref, out_ref):
+    rows = groups_ref.shape[0]
+    lanes = lax.broadcasted_iota(jnp.int32, (rows, 128), 1)
+    steps = step_ref[...].astype(F32)
+    for core in range(2):
+        for t in range(8):
+            here = slice((8 * core + t) * rows, (8 * core + t + 1) * rows)
+            column = 0
+            for ref in (groups_ref, input_ref, gate_ref):
+                width = ref.shape[1] // 16
+                first = (2 * t + core) * width
+                out_ref[here, column : column + width] = ref[:, first : first + width]
+                column += width
+            turned = pltpu.roll(steps, (128 - HEADS * t) % 128, 1) if t else steps
+            mine = (lanes >= 8 * core) & (lanes < 8 * core + 8)
+            out_ref[here, column:] = jnp.where(mine, turned, 0.0).astype(BF16)
+
+
+def deal(groups, inputs, gates, steps):
+    return pl.pallas_call(
+        deal_kernel,
+        out_shape=jax.ShapeDtypeStruct((16 * groups.shape[0], WIDTH + 128), BF16),
+        compiler_params=pltpu.CompilerParams(vmem_limit_bytes=16 * 1024 * 1024),
+        name="deal",
+    )(groups, inputs, gates, steps)
+
+
 def assemble_kernel(blocks_ref, out_ref):
     out_ref[:KB, :] = blocks_ref[:, :WIDTH]
     out_ref[KB:, :] = jnp.zeros((16, WIDTH), BF16)
@@ -64,82 +91,97 @@
     )(blocks)
 
 
-def project_kernel(steps, last, table, own_ref, oth_ref, *refs):
-    pieces, refs = refs[:5], refs[5:]
-    sums, refs = (refs[:2], refs[2:]) if last else ((None, None), refs)
-    out_own, out_oth, weights, turned = refs
-    step = pl.program_id(0)
-    tiles = pl.num_programs(0) // 2
+def project_kernel(steps, counts, last, table, own_hbm, oth_hbm, *refs):
+    pieces, refs = list(refs[: sum(counts)]), refs[sum(counts) :]
+    parts = [[pieces.pop(0) for _ in range(count)] for count in counts]
+    final = len(parts) - 1
+    sums, refs = (refs[:2], refs[2:]) if last else ((), refs)
+    outs, (hid, weights, totals, results, sems) = refs[:2], refs[2:]
+    rows = own_hbm.shape[0]
+    width = weights.shape[2]
     half = KB // 2
-
-    @pl.when(step == 0)
-    def _():
-        for ref, block, skip, rows in zip(pieces, (0, 1, 2, 2, 3), (0, 0, 0, half, 0), (KB, KB, half, half, KB)):
-            start = pl.multiple_of(table[1 + block] * KB + skip, half)
-            weights[pl.ds(start, rows), :] = ref[:rows, :]
-            if steps and ref.shape[0] > rows:
-                start = pl.multiple_of(table[1 + block] * KB, KB)
-                turned[:, pl.ds(start, KB)] = ref[rows:, :KB]
-
-    def run(hid_ref, sum_ref, out_ref):
-        hid = hid_ref[...]
-        width = weights.shape[1]
-        total = jnp.dot(hid, weights[...], preferred_element_type=F32)
-        if last:
-            total = total + sum_ref[:, :width]
-        out_ref[:, :width] = total.astype(out_ref.dtype)
-        if steps:
-            extra = lax.dot_general(hid, turned[...], NT, preferred_element_type=F32)
-            if last:
-                extra = extra + sum_ref[:, width : width + steps]
-            out_ref[:, width:] = jnp.zeros((out_ref.shape[0], out_ref.shape[1] - width), out_ref.dtype)
-            out_ref[:, width : width + steps] = extra.astype(out_ref.dtype)
-
-    @pl.when(step < tiles)
-    def _():
-        run(own_ref, sums[0], out_own)
-
-    @pl.when(step >= tiles)
-    def _():
-        run(oth_ref, sums[1], out_oth)
-
-
-def project_part(own, oth, pieces, dy, steps=0, sums=()):
-    rows, depth = own.shape[0], own.shape[1] // 2
-    pieces = [part for piece in pieces for part in (piece if isinstance(piece, tuple) else (piece,))]
+    fetches = []
+    for at, part in enumerate(parts):
+        start = pl.multiple_of(table[at] * KB, KB)
+        copies = [
+            pltpu.make_async_copy(src.at[:, pl.ds(start, KB)], hid.at[at, which], sems.at[at, which])
+            for which, src in enumerate((own_hbm, oth_hbm))
+        ]
+        for which, src in enumerate(part):
+            into = weights.at[at, pl.ds(which * half, src.shape[0])]
+            copies.append(pltpu.make_async_copy(src, into, sems.at[at, 2 + which]))
+        fetches.append(copies)
+        for copy in copies:
+            copy.start()
+    if last:
+        fetches.append([pltpu.make_async_copy(src, totals.at[1, which], sems.at[len(parts), which]) for which, src in enumerate(sums)])
+        for copy in fetches[-1]:
+            copy.start()
+    tile = 256
+    stores = []
+    for at in range(len(parts)):
+        for copy in fetches[at]:
+            copy.wait()
+        if last and at == final:
+            for copy in fetches[-1]:
+                copy.wait()
+        for which in (1, 0):
+            for first in range(0, rows, tile):
+                here = pl.ds(first, tile)
+                block = hid[at, which, here]
+                main = jnp.dot(block, weights[at, :KB], preferred_element_type=F32)
+                extra = lax.dot_general(block, weights[at, KB:, :KB], NT, preferred_element_type=F32)
+                extra = jnp.concatenate([extra, jnp.zeros((tile, 128 - steps), F32)], axis=1)
+                if at:
+                    main += totals[0, which, here, :width]
+                    extra += totals[0, which, here, width:]
+                if at < final:
+                    totals[0, which, here, :width] = main
+                    totals[0, which, here, width:] = extra
+                else:
+                    if last:
+                        main += totals[1, which, here, :width]
+                        extra += totals[1, which, here, width:]
+                    results[which, here, :width] = main.astype(results.dtype)
+                    results[which, here, width:] = extra.astype(results.dtype)
+            if at == final:
+                stores.append(pltpu.make_async_copy(results.at[which], outs[which], sems.at[len(parts) + 1, which]))
+                stores[-1].start()
+    for store in stores:
+        store.wait()
+
+
+def project_part(own, oth, pieces, steps, sums=()):
+    rows, depth = own.shape
+    x, yh = lax.axis_index("x"), lax.axis_index("yh")
+    table = jnp.stack([4 * ((yh + dy) % 2) + (x + dx) % 4 for (dy, dx), _ in pieces]).astype(jnp.int32)
+    pieces = [piece if isinstance(piece, tuple) else (piece,) for _, piece in pieces]
+    counts = [len(piece) for piece in pieces]
+    pieces = [part for piece in pieces for part in piece]
     width = pieces[0].shape[1]
-    out_width = width + (128 if steps else 0)
-    tile = 256
-    tiles = rows // tile
-    x = lax.axis_index("x")
-    yh = (lax.axis_index("yh") + dy) % 2
-    table = jnp.stack([yh] + [(x + dx) % 4 for dx in range(4)]).astype(jnp.int32)
-
-    def first(i, _):
-        return (jnp.minimum(i, tiles - 1), 0)
-
-    def second(i, _):
-        return (jnp.maximum(i - tiles, 0), 0)
-
-    outs = [pl.BlockSpec((tile, out_width), first), pl.BlockSpec((tile, out_width), second)]
+    out_width = width + 128
+    dtype = BF16 if sums else F32
     return pl.pallas_call(
-        functools.partial(project_kernel, steps, bool(sums)),
+        functools.partial(project_kernel, steps, counts, bool(sums)),
         grid_spec=pltpu.PrefetchScalarGridSpec(
             num_scalar_prefetch=1,
-            grid=(2 * tiles,),
-            in_specs=[
-                pl.BlockSpec((tile, depth), lambda i, t: (jnp.minimum(i, tiles - 1), t[0])),
-                pl.BlockSpec((tile, depth), lambda i, t: (jnp.maximum(i - tiles, 0), t[0])),
-            ]
-            + [pl.BlockSpec(p.shape, lambda i, _: (0, 0)) for p in pieces]
-            + (outs if sums else []),
-            out_specs=outs,
-            scratch_shapes=[pltpu.VMEM((depth, width), BF16), pltpu.VMEM((16, depth), BF16)],
+            grid=(1,),
+            in_specs=[pl.BlockSpec(memory_space=pl.ANY)] * (2 + len(pieces) + len(sums)),
+            out_specs=[pl.BlockSpec(memory_space=pl.ANY)] * 2,
+            scratch_shapes=[
+                pltpu.VMEM((len(counts), 2, rows, KB), BF16),
+                pltpu.VMEM((len(counts), KB + 16, width), BF16),
+                pltpu.VMEM((2 if sums else 1, 2, rows, out_width), F32),
+                pltpu.VMEM((2, rows, out_width), dtype),
+                pltpu.SemaphoreType.DMA((len(counts) + 2, 4)),
+            ],
         ),
-        out_shape=[jax.ShapeDtypeStruct((rows, out_width), BF16 if sums else F32)] * 2,
+        out_shape=[jax.ShapeDtypeStruct((rows, out_width), dtype)] * 2,
         compiler_params=pltpu.CompilerParams(vmem_limit_bytes=FAST),
         cost_estimate=pl.CostEstimate(
-            flops=4 * rows * depth * width, bytes_accessed=4 * rows * depth + 2 * depth * width, transcendentals=0
+            flops=4 * rows * KB * width * len(counts),
+            bytes_accessed=2 * KB * (2 * rows + width) * len(counts) + 12 * rows * width,
+            transcendentals=0,
         ),
         name="project",
     )(table, own, oth, *pieces, *sums)
@@ -198,7 +240,7 @@
     x_t = x.T
     init_all = init[...].reshape(CH, N)
     carried = lax.dot_general(init_all.astype(BF16), c, NT, preferred_element_type=F32)
-    parts = []
+    parts, kept = [], []
     for h in range(HEADS):
         at = slice(h * P_SIZE, (h + 1) * P_SIZE)
         decay = jnp.exp(jnp.minimum(total_t[h : h + 1, :] - total[:, h : h + 1], 0.0))
@@ -206,8 +248,10 @@
         weighted = (x_t[at] * step_t[h : h + 1, :]).astype(BF16)
         inner = jnp.dot(weighted, mixing, preferred_element_type=F32)
         parts.append(inner + carried[at] * grow_t[h : h + 1, :])
-        kept = (x_t[at] * rest_t[h : h + 1, :]).astype(BF16)
-        final_ref[0, h] = init[0, h] * end[h : h + 1, :] + jnp.dot(kept, b, preferred_element_type=F32)
+        kept.append((x_t[at] * rest_t[h : h + 1, :]).astype(BF16))
+    added = jnp.dot(jnp.concatenate(kept, axis=0), b, preferred_element_type=F32)
+    for h in range(HEADS):
+        final_ref[0, h] = init[0, h] * end[h : h + 1, :] + added[h * P_SIZE : (h + 1) * P_SIZE]
     y = jnp.concatenate(parts, axis=0).T
     y = y + skip[...] * x
     low = y[:, :HALF] * silu(jnp.where(first, zo_v, zr_v))
@@ -295,44 +339,27 @@
     for dz in range(4):
         for f, ref in enumerate((own_ref, oth_ref)):
             rows[(2 * dz + f) * per : (2 * dz + f + 1) * per, :] = ref[dz * per : (dz + 1) * per, :]
-    depth = rows.shape[1]
-    for which, out_ref in ((pieces[:split], first_ref), (pieces[split:], second_ref)):
-        column = 0
-        at = 0
-        while at < len(which):
-            ref = which[at]
-            width = ref.shape[1]
-            if ref.shape[0] == depth:
-                total = jnp.dot(rows[...], ref[...], preferred_element_type=F32)
-                at += 1
-            else:
-                total = jnp.dot(rows[:, : depth // 2], ref[...], preferred_element_type=F32)
-                total += jnp.dot(rows[:, depth // 2 :], which[at + 1][...], preferred_element_type=F32)
-                at += 2
-            out_ref[:, column : column + width] = total.astype(BF16)
-            column += width
+    width = pieces[0].shape[1]
+    for at, ref in enumerate(pieces):
+        out_ref, column = (first_ref, at * width) if at < split else (second_ref, (at - split) * width)
+        total = jnp.dot(rows[...], ref[...], preferred_element_type=F32)
+        out_ref[:, column : column + width] = total.astype(BF16)
 
 
 def multiply(own, oth, first, second):
     rows, depth = own.shape
-
-    def flat(pieces):
-        return [part for piece in pieces for part in (piece if isinstance(piece, tuple) else (piece,))]
-
-    def columns(pieces):
-        return sum(p[0].shape[1] if isinstance(p, tuple) else p.shape[1] for p in pieces)
-
-    total = columns(first) + columns(second)
+    columns = [len(pieces) * pieces[0].shape[1] for pieces in (first, second)]
+    total = sum(columns)
     return pl.pallas_call(
-        functools.partial(multiply_kernel, len(flat(first))),
-        out_shape=[jax.ShapeDtypeStruct((2 * rows, columns(p)), BF16) for p in (first, second)],
+        functools.partial(multiply_kernel, len(first)),
+        out_shape=[jax.ShapeDtypeStruct((2 * rows, n), BF16) for n in columns],
         scratch_shapes=[pltpu.VMEM((2 * rows, depth), BF16)],
         compiler_params=pltpu.CompilerParams(vmem_limit_bytes=36 * 1024 * 1024),
         cost_estimate=pl.CostEstimate(
             flops=4 * rows * depth * total, bytes_accessed=4 * rows * depth + 2 * total * (depth + 2 * rows), transcendentals=0
         ),
         name="multiply",
-    )(own, oth, *flat(first), *flat(second))
+    )(own, oth, *first, *second)
 
 
 def add(*terms):
@@ -388,30 +415,29 @@
     yh, x, c = lax.axis_index("yh"), lax.axis_index("x"), lax.axis_index("c")
     yl, z = lax.axis_index("yl"), lax.axis_index("z")
     group = ("c", "yl", "z")
-    rows = w_gate.shape[0]
-
-    def by_owner(weight):
-        width = weight.shape[1] // 16
-        return weight.reshape(rows, 8, 2, width).transpose(2, 1, 0, 3).reshape(16 * rows, width)
-
-    steps = by_owner(w_step).reshape(2, 8 * rows, 8)
-    steps = jnp.concatenate([jnp.pad(steps[core], ((0, 0), (8 * core, 120 - 8 * core))) for core in range(2)])
-    blocks = jnp.concatenate([by_owner(w_groups), by_owner(w_input), by_owner(w_gate), steps], axis=1)
+    blocks = deal(w_groups, w_input, w_gate, w_step)
     s_own = assemble(lax.all_to_all(blocks, group, 0, 0, tiled=True))
     hidden_oth = swap(hidden_in, "c")
 
     half = KB // 2
-    w_r, w_l, w_o = right(w_out), left(w_out), over(w_out)
-    s_r, s_l, s_o = right(s_own, w_r, w_l), left(s_own, w_r, w_l), over(s_own, w_o)
+    w_r, w_l = right(w_out), left(w_out)
+    w_f = lax.ppermute(w_out, "x", ring(4, 2))
+    s_r, s_l, s_o = right(s_own, w_r, w_l, w_f), left(s_own, w_r, w_l, w_f), over(s_own)
+    w_o = over(w_out, s_o)
     s_ft, s_fb = right(s_r[:half], s_l), left(s_l[half:], s_r)
-    near = project_part(hidden_in, hidden_oth, [s_own, s_l, (s_ft, s_fb), s_r], 0, 16)
-    s_or, s_ol = right(s_o, s_ft, s_fb), left(s_o, s_ft, s_fb)
+    near = project_part(
+        hidden_in,
+        hidden_oth,
+        [((0, 0), s_own), ((0, 1), s_l), ((0, 3), s_r), ((1, 0), s_o), ((0, 2), (s_ft, s_fb))],
+        16,
+    )
+    s_or, s_ol = right(s_o, s_ft, s_fb, w_o), left(s_o, s_ft, s_fb, w_o)
     s_oft, s_ofb = over(s_ft), over(s_fb)
-    own, oth = project_part(hidden_in, hidden_oth, [s_o, s_ol, (s_oft, s_ofb), s_or], 1, 16, near)
-    w_ft, w_fb = right(w_r[:KB], s_or, s_ol), left(w_l[KB:], s_or, s_ol)
-    w_or, w_ol = right(w_o, s_or, s_ol), left(w_o, s_or, s_ol)
-    w_oft, w_ofb = over(w_ft, s_oft, s_ofb), over(w_fb, s_oft, s_ofb)
-    got = swap(after(oth, w_ft, w_fb), "c")
+    own, oth = project_part(
+        hidden_in, hidden_oth, [((1, 1), s_ol), ((1, 3), s_or), ((1, 2), (s_oft, s_ofb))], 16, near
+    )
+    w_or, w_ol, w_of = right(w_o, s_or, s_ol), left(w_o, s_or, s_ol), over(w_f, s_oft, s_ofb)
+    got = swap(oth, "c")
 
     def lanes(vector):
         return jnp.pad(vector, (0, 128 - HEADS))[None, :]
@@ -432,11 +458,9 @@
         jnp.repeat(skip_gain, P_SIZE)[None, :],
         norm_gain[None, :],
     )
-    normed_oth = swap(after(normed, w_or, w_ol, w_oft, w_ofb), "c")
-
-    first, second = multiply(
-        normed, normed_oth, [w_out, w_l, w_r, w_o], [(w_ft, w_fb), w_ol, (w_oft, w_ofb), w_or]
-    )
+    normed_oth = swap(after(normed, w_or, w_ol, w_of), "c")
+
+    first, second = multiply(normed, normed_oth, [w_out, w_l, w_r, w_o], [w_f, w_ol, w_of, w_or])
     first, second = reduce_yl_first(first), reduce_z_first(second)
     sums = jnp.concatenate([first, second], axis=2)
     kept = sums[0]

time: 211 us -> 208 us (0.986)
  Pallas kernels: 43.3 us -> 39.5 us
  local copies, waits for them, and re-layouts: 9.56 us -> 12.8 us
  starting transfers between devices: 55.3 us -> 52.1 us
    ppermute x6 -> x5, waiting for transfers between devices: 11.4 us -> 26.3 us  [left(): return lax.ppermute(after(value, *others), 'x', ring(4, -1))]
    ppermute x6 -> x5, waiting for transfers between devices: 17.5 us -> 3.74 us  [right(): return lax.ppermute(after(value, *others), 'x', ring(4, 1))]
    unnamed x31 -> x52, local copies, waits for them, and re-layouts: 4.7 us -> 12 us
    ppermute x6 -> x5, starting transfers between devices: 12.5 us -> 5.69 us  [left(): return lax.ppermute(after(value, *others), 'x', ring(4, -1))]
    ppermute x0 -> x1, waiting for transfers between devices: none -> 6.45 us  [shards(): w_f = lax.ppermute(w_out, 'x', ring(4, 2))]
    ppermute x12 -> x11, waiting for transfers between devices: 31.1 us -> 25.7 us  [swap(): return lax.ppermute(value, axis, [(0, 1), (1, 0)])]
    pallas_call x3 -> x4, Pallas kernels: 31.4 us -> 27.7 us  [the longest x2 20.7 us: project_part(): pl.pallas_call(functools.partial(project_kernel, steps, counts, bool(sums...]
    ppermute x12 -> x11, starting transfers between devices: 20.9 us -> 22.7 us  [swap(): return lax.ppermute(value, axis, [(0, 1), (1, 0)])]
  transfers between devices with their start and end apart: 33 -> 31, of which waited for: 16 -> 15; matrix products, arithmetic and copies ran while one was open for 1% -> 1% of each run, Pallas kernels for 17% -> 12%
where the time goes in v1:
time: 208 us; the launch traced here: 207 us
  waiting for transfers between devices  100 us (48%)
  starting transfers between devices  52.1 us (25%)
  Pallas kernels  39.5 us (19%)
  local copies, waits for them, and re-layouts  12.8 us (6%)
    ppermute x5, waiting for transfers between devices, left(): return lax.ppermute(after(value, *others), 'x', ring(4, -1))  26.3 us
    ppermute x11, waiting for transfers between devices, swap(): return lax.ppermute(value, axis, [(0, 1), (1, 0)])  25.7 us
    ppermute x11, starting transfers between devices, swap(): return lax.ppermute(value, axis, [(0, 1), (1, 0)])  22.7 us
    pallas_call x2, Pallas kernels, project_part(): pl.pallas_call(functools.partial(project_kernel, steps, counts, bool(sums...  20.7 us
    all_to_all x1, waiting for transfers between devices, shards(): s_own = assemble(lax.all_to_all(blocks, group, 0, 0, tiled=True))  16.2 us
    ppermute x2, waiting for transfers between devices, reduce_z(): from_below = lax.ppermute(up, 'z', ring(4, 1))  14 us
    unnamed x52, local copies, waits for them, and re-layouts  12 us
    pallas_call x1, Pallas kernels, scan(): pl.pallas_call(scan_kernel, grid_spec=pltpu.PrefetchScalarGridSpec(num_sc...  10.3 us
  transfers between devices with their start and end apart: 31, of which 15 were waited for; matrix products, arithmetic and copies ran while one was open for 1% of the time, Pallas kernels for 12%

profile of v1, /device:TPU:1, one launch (start us, length us, event | category | flops | bytes accessed | tf_op | source)
XLA Modules:
  0.0 207.1 jit_solution(10458281650771088862)
XLA Ops:
  7.1 6.7 %all-to-all-start = ((bf16[16,32,1408]{2,1,0:T(8,128)(2,1)}), bf16[16,32,1408]{2,1,0:T(8,128)(2,1)S(1)}, u32[]{:S(2)}, u32[]{:S(2)}) async-start(bf16[16,32,1408]{2,1,0:T(8,128)(2,1)} %bitcast.20), calls=%async_computation | async-start | bytes 2883584 | tf_op jit(solution)/shard_map/all_to_all | solution.py:419
  18.1 16.2 %all-to-all-done = bf16[16,32,1408]{2,1,0:T(8,128)(2,1)S(1)} async-done(((bf16[16,32,1408]{2,1,0:T(8,128)(2,1)}), bf16[16,32,1408]{2,1,0:T(8,128)(2,1)S(1)}, u32[]{:S(2)}, u32[]{:S(2)}) %all-to-all-start) | async-done | bytes 1441824 | tf_op jit(solution)/shard_map/all_to_all | solution.py:419
  34.4 6.5 %collective-permute-done.4.refs_4_ = bf16[1024,256]{1,0:T(8,128)(2,1)} collective-permute-done((bf16[1024,256]{1,0:T(8,128)(2,1)S(1)}, bf16[1024,256]{1,0:T(8,128)(2,1)}, u32[]{:S(2)}, u32[]{:S(2)}) %collective-permute-start.4) | collective-permute-done | bytes 524320 | tf_op jit(solution)/shard_map/ppermute | solution.py:424
  42.3 2.6 %collective-permute-start.1 = (bf16[528,1280]{1,0:T(8,128)(2,1)S(1)}, bf16[528,1280]{1,0:T(8,128)(2,1)}, u32[]{:S(2)}, u32[]{:S(2)}) collective-permute-start(bf16[528,1280]{1,0:T(8,128)(2,1)S(1)} %assemble.1.refs_0_), channel_id=1, source_target_pairs={{0,64},{64,0},{1,65},{65,1},{2,66},{66,2},{3,67},{67,3},{4,68},{68... | collective-permute-start | bytes 4055048 | tf_op jit(solution)/shard_map/ppermute | solution.py:32
  44.9 26.3 %collective-permute-done.6.refs_1_ = bf16[528,1280]{1,0:T(8,128)(2,1)S(1)} collective-permute-done((bf16[528,1280]{1,0:T(8,128)(2,1)S(1)}, bf16[528,1280]{1,0:T(8,128)(2,1)S(1)}, u32[]{:S(2)}, u32[]{:S(2)}) %collective-permute-start.6) | collective-permute-done | bytes 1351712 | tf_op jit(solution)/shard_map/ppermute | solution.py:44
  75.4 2.5 %collective-permute-start.9 = (bf16[1024,256]{1,0:T(8,128)(2,1)S(1)}, bf16[1024,256]{1,0:T(8,128)(2,1)S(1)}, u32[]{:S(2)}, u32[]{:S(2)}) collective-permute-start(bf16[1024,256]{1,0:T(8,128)(2,1)S(1)} %copy-done.12), channel_id=1, source_target_pairs={{0,64},{64,0},{1,65},{65,1},{2,66},{66,2},{3,67},{67,3},{4,68},{68... | collective-permute-start | bytes 1572872 | tf_op jit(solution)/shard_map/ppermute | solution.py:32
  77.9 9.3 %collective-permute-done.9.refs_3_ = bf16[1024,256]{1,0:T(8,128)(2,1)S(1)} collective-permute-done((bf16[1024,256]{1,0:T(8,128)(2,1)S(1)}, bf16[1024,256]{1,0:T(8,128)(2,1)S(1)}, u32[]{:S(2)}, u32[]{:S(2)}) %collective-permute-start.9) | collective-permute-done | bytes 524320 | tf_op jit(solution)/shard_map/ppermute | solution.py:32
  91.7 2.4 %collective-permute-start.12 = (bf16[256,1280]{1,0:T(8,128)(2,1)}, bf16[256,1280]{1,0:T(8,128)(2,1)}, u32[]{:S(2)}, u32[]{:S(2)}) collective-permute-start(bf16[256,1280]{1,0:T(8,128)(2,1)} %collective-permute-done.7.refs_4_), channel_id=1, source_target_pairs={{0,64},{64,0},{1,65},{65,1},{2,66},{66,2},{3,67},{67,3},{4,68},{68... | collective-permute-start | bytes 1966088 | tf_op jit(solution)/shard_map/ppermute | solution.py:32
  98.6 12.8 %project.2 = (f32[512,1408]{1,0:T(8,128)}, f32[512,1408]{1,0:T(8,128)}) custom-call(s32[5]{0:T(128)S(1)} %stack.107.table, bf16[512,4096]{1,0:T(8,128)(2,1)} %own_hbm.3, bf16[512,4096]{1,0:T(8,128)(2,1)} %collective-permute-done.oth_hbm, bf16[528,1280]{1,0:T(8,128)(2,1)S(1)} %assemble.1.refs_0_, bf16[528,1280]{1,0:T(8,128)(2,1)S(1)} %copy-done.3, ...), custom_call_target="tpu_custom_call" | custom-call | flops 6710886400 | bytes 19660800 | tf_op jit(solution)/shard_map/project/pallas_call | solution.py:164
  111.4 9.1 %collective-permute-done.13.refs_3_ = bf16[272,1280]{1,0:T(8,128)(2,1)S(1)} collective-permute-done((bf16[272,1280]{1,0:T(8,128)(2,1)}, bf16[272,1280]{1,0:T(8,128)(2,1)S(1)}, u32[]{:S(2)}, u32[]{:S(2)}) %collective-permute-start.13) | collective-permute-done | bytes 696352 | tf_op jit(solution)/shard_map/ppermute | solution.py:32
  120.7 7.8 %project.3 = (bf16[512,1408]{1,0:T(8,128)(2,1)S(1)}, bf16[512,1408]{1,0:T(8,128)(2,1)}) custom-call(s32[3]{0:T(128)S(1)} %pad_add_fusion.1.table, bf16[512,4096]{1,0:T(8,128)(2,1)} %own_hbm.3, bf16[512,4096]{1,0:T(8,128)(2,1)} %collective-permute-done.oth_hbm, bf16[528,1280]{1,0:T(8,128)(2,1)S(1)} %collective-permute-done.10.refs_0_, ...), custom_call_target="tpu_custom_call" | custom-call | flops 4026531840 | bytes 14942208 | tf_op jit(solution)/shard_map/project/pallas_call | solution.py:164
  129.6 4.9 %collective-permute-start.14 = (bf16[512,1408]{1,0:T(8,128)(2,1)}, bf16[512,1408]{1,0:T(8,128)(2,1)S(1)}, u32[]{:S(2)}, u32[]{:S(2)}) collective-permute-start(bf16[512,1408]{1,0:T(8,128)(2,1)} %get-tuple-element.26), channel_id=1, source_target_pairs={{0,8},{8,0},{1,9},{9,1},{2,10},{10,2},{3,11},{11,3},{4,12},{12,4},... | collective-permute-start | bytes 4325384 | tf_op jit(solution)/shard_map/ppermute | solution.py:32
  134.7 2.4 %collective-permute-start.17 = (bf16[1024,256]{1,0:T(8,128)(2,1)}, bf16[1024,256]{1,0:T(8,128)(2,1)S(1)}, u32[]{:S(2)}, u32[]{:S(2)}) collective-permute-start(bf16[1024,256]{1,0:T(8,128)(2,1)} %collective-permute-done.4.refs_4_), channel_id=1, source_target_pairs={{0,64},{64,0},{1,65},{65,1},{2,66},{66,2},{3,67},{67,3},{4,68},{68... | collective-permute-start | bytes 1572872 | tf_op jit(solution)/shard_map/ppermute | solution.py:32
  137.1 2.7 %collective-permute-start.16 = (bf16[1024,256]{1,0:T(8,128)(2,1)}, bf16[1024,256]{1,0:T(8,128)(2,1)S(1)}, u32[]{:S(2)}, u32[]{:S(2)}) collective-permute-start(bf16[1024,256]{1,0:T(8,128)(2,1)} %copy-done.14), channel_id=1, source_target_pairs={{0,48},{16,0},{32,16},{48,32},{1,49},{17,1},{33,17},{49,33},{2,50}... | collective-permute-start | bytes 1572872 | tf_op jit(solution)/shard_map/ppermute | solution.py:44
  141.3 10.3 %scan.1 = (bf16[512,1024]{1,0:T(8,128)(2,1)S(1)}, f32[4,16,64,256]{3,2,1,0:T(8,128)}) custom-call(s32[13]{0:T(128)S(1)} %pad_add_fusion.info, bf16[512,1408]{1,0:T(8,128)(2,1)S(1)} %copy-done.9, bf16[512,1408]{1,0:T(8,128)(2,1)S(1)} %collective-permute-done.14.got, bf16[4,3,1024]{2,1,0:T(4,128)(2,1)S(1)} %copy.21.tail_x, ...), custom_call_target="tpu_custom_call" | custom-call | flops 2000000000 | bytes 14000000 | tf_op jit(solution)/shard_map/scan/pallas_call | solution.py:279
  155.2 5.8 %multiply.1 = (bf16[1024,1024]{1,0:T(8,128)(2,1)S(1)}, bf16[1024,1024]{1,0:T(8,128)(2,1)S(1)}) custom-call(bf16[512,1024]{1,0:T(8,128)(2,1)S(1)} %get-tuple-element.30.own_ref, bf16[512,1024]{1,0:T(8,128)(2,1)S(1)} %collective-permute-done.18.oth_ref, bf16[1024,256]{1,0:T(8,128)(2,1)S(1)} %copy-done.13, bf16[1024,256]{1,0:T(8,128)(2,1)} %collective-permute-done.3.refs_1_, ...), custom_call_target="tpu_custom_call" | custom-call | flops 4294967296 | bytes 10485760 | tf_op jit(solution)/shard_map/multiply/pallas_call | solution.py:353
  164.2 5.8 %collective-permute-done.24 = bf16[256,512]{1,0:T(8,128)(2,1)S(1)} collective-permute-done((bf16[256,512]{1,0:T(8,128)(2,1)S(1)}, bf16[256,512]{1,0:T(8,128)(2,1)S(1)}, u32[]{:S(2)}, u32[]{:S(2)}) %collective-permute-start.24) | collective-permute-done | bytes 262176 | tf_op jit(solution)/shard_map/ppermute | solution.py:372
  170.3 2.7 %collective-permute-start.27 = (bf16[256,1024]{1,0:T(8,128)(2,1)S(1)}, bf16[256,1024]{1,0:T(8,128)(2,1)S(1)}, u32[]{:S(2)}, u32[]{:S(2)}) collective-permute-start(bf16[256,1024]{1,0:T(8,128)(2,1)S(1)} %pad_maximum_fusion.1), channel_id=1, source_target_pairs={{0,3},{1,0},{2,1},{3,2},{4,7},{5,4},{6,5},{7,6},{8,11},{9,8},{10,9... | collective-permute-start | bytes 1572872 | tf_op jit(solution)/shard_map/ppermute | solution.py:378
  173.0 10.6 %collective-permute-done.25 = bf16[256,1024]{1,0:T(8,128)(2,1)S(1)} collective-permute-done((bf16[256,1024]{1,0:T(8,128)(2,1)S(1)}, bf16[256,1024]{1,0:T(8,128)(2,1)S(1)}, u32[]{:S(2)}, u32[]{:S(2)}) %collective-permute-start.25) | collective-permute-done | bytes 524320 | tf_op jit(solution)/shard_map/ppermute | solution.py:377
  183.9 3.9 %collective-permute-done.19 = bf16[8,64,1024]{2,1,0:T(8,128)(2,1)S(1)} collective-permute-done((bf16[8,64,1024]{2,1,0:T(8,128)(2,1)S(1)}, bf16[8,64,1024]{2,1,0:T(8,128)(2,1)S(1)}, u32[]{:S(2)}, u32[]{:S(2)}) %collective-permute-start.19) | collective-permute-done | bytes 1048608 | tf_op jit(solution)/shard_map/ppermute | solution.py:32
  188.7 2.7 %collective-permute-start.22 = (bf16[128,512]{1,0:T(8,128)(2,1)S(1)}, bf16[128,512]{1,0:T(8,128)(2,1)S(1)}, u32[]{:S(2)}, u32[]{:S(2)}) collective-permute-start(bf16[128,512]{1,0:T(8,128)(2,1)S(1)} %get-tuple-element.47), channel_id=1, source_target_pairs={{0,3},{1,0},{2,1},{3,2},{4,7},{5,4},{6,5},{7,6},{8,11},{9,8},{10,9... | collective-permute-start | bytes 393224 | tf_op jit(solution)/shard_map/ppermute | solution.py:373
  193.7 2.9 %collective-permute-start.23 = (bf16[128,1024]{1,0:T(8,128)(2,1)S(1)}, bf16[128,1024]{1,0:T(8,128)(2,1)S(1)}, u32[]{:S(2)}, u32[]{:S(2)}) collective-permute-start(bf16[128,1024]{1,0:T(8,128)(2,1)S(1)} %pad_maximum_fusion.4), channel_id=1, source_target_pairs={{0,3},{1,0},{2,1},{3,2},{4,7},{5,4},{6,5},{7,6},{8,11},{9,8},{10,9... | collective-permute-start | bytes 786440 | tf_op jit(solution)/shard_map/ppermute | solution.py:378
  196.7 3.4 %collective-permute-done.21 = bf16[128,1024]{1,0:T(8,128)(2,1)S(1)} collective-permute-done((bf16[128,1024]{1,0:T(8,128)(2,1)S(1)}, bf16[128,1024]{1,0:T(8,128)(2,1)S(1)}, u32[]{:S(2)}, u32[]{:S(2)}) %collective-permute-start.21) | collective-permute-done | bytes 262176 | tf_op jit(solution)/shard_map/ppermute | solution.py:377
  200.2 4.3 %collective-permute-start.29 = (bf16[64,2048]{1,0:T(8,128)(2,1)S(1)}, bf16[64,2048]{1,0:T(8,128)(2,1)S(1)}, u32[]{:S(2)}, u32[]{:S(2)}) collective-permute-start(bf16[64,2048]{1,0:T(8,128)(2,1)S(1)} %get-tuple-element.44), channel_id=1, source_target_pairs={{0,8},{8,0},{1,9},{9,1},{2,10},{10,2},{3,11},{11,3},{4,12},{12,4},... | collective-permute-start | bytes 786440 | tf_op jit(solution)/shard_map/ppermute | solution.py:32
  (126 shorter events, 41.3 us)
Async XLA Ops:
  0.6 94.2 %collective-permute-start = (bf16[512,4096]{1,0:T(8,128)(2,1)}, bf16[512,4096]{1,0:T(8,128)(2,1)}, u32[]{:S(2)}, u32[]{:S(2)}) collective-permute-start(bf16[512,4096]{1,0:T(8,128)(2,1)} %own_hbm.3), channel_id=1, source_target_pairs={{0,8},{8,0},{1,9},{9,1},{2,10},{10,2},{3,11},{11,3},{4,12},{12,4},... | collective-permute-start | bytes 12582920 | tf_op jit(solution)/shard_map/ppermute | solution.py:32
  7.1 27.2 %all-to-all-start = ((bf16[16,32,1408]{2,1,0:T(8,128)(2,1)}), bf16[16,32,1408]{2,1,0:T(8,128)(2,1)S(1)}, u32[]{:S(2)}, u32[]{:S(2)}) async-start(bf16[16,32,1408]{2,1,0:T(8,128)(2,1)} %bitcast.20), calls=%async_computation | async-start | bytes 2883584 | tf_op jit(solution)/shard_map/all_to_all | solution.py:419
  13.8 20.6 %collective-permute-start.2 = (bf16[1024,256]{1,0:T(8,128)(2,1)S(1)}, bf16[1024,256]{1,0:T(8,128)(2,1)}, u32[]{:S(2)}, u32[]{:S(2)}) collective-permute-start(bf16[1024,256]{1,0:T(8,128)(2,1)S(1)} %copy-done.12), channel_id=1, source_target_pairs={{0,16},{16,32},{32,48},{48,0},{1,17},{17,33},{33,49},{49,1},{2,18}... | collective-permute-start | bytes 1572872 | tf_op jit(solution)/shard_map/ppermute | solution.py:40
  15.1 19.3 %collective-permute-start.3 = (bf16[1024,256]{1,0:T(8,128)(2,1)S(1)}, bf16[1024,256]{1,0:T(8,128)(2,1)}, u32[]{:S(2)}, u32[]{:S(2)}) collective-permute-start(bf16[1024,256]{1,0:T(8,128)(2,1)S(1)} %copy-done.12), channel_id=1, source_target_pairs={{0,48},{16,0},{32,16},{48,32},{1,49},{17,1},{33,17},{49,33},{2,50}... | collective-permute-start | bytes 1572872 | tf_op jit(solution)/shard_map/ppermute | solution.py:44
  16.5 24.3 %collective-permute-start.4 = (bf16[1024,256]{1,0:T(8,128)(2,1)S(1)}, bf16[1024,256]{1,0:T(8,128)(2,1)}, u32[]{:S(2)}, u32[]{:S(2)}) collective-permute-start(bf16[1024,256]{1,0:T(8,128)(2,1)S(1)} %copy-done.12), channel_id=1, source_target_pairs={{0,32},{16,48},{32,0},{48,16},{1,33},{17,49},{33,1},{49,17},{2,34}... | collective-permute-start | bytes 1572872 | tf_op jit(solution)/shard_map/ppermute | solution.py:424
  40.9 30.4 %collective-permute-start.6 = (bf16[528,1280]{1,0:T(8,128)(2,1)S(1)}, bf16[528,1280]{1,0:T(8,128)(2,1)S(1)}, u32[]{:S(2)}, u32[]{:S(2)}) collective-permute-start(bf16[528,1280]{1,0:T(8,128)(2,1)S(1)} %assemble.1.refs_0_), channel_id=1, source_target_pairs={{0,48},{16,0},{32,16},{48,32},{1,49},{17,1},{33,17},{49,33},{2,50}... | collective-permute-start | bytes 4055048 | tf_op jit(solution)/shard_map/ppermute | solution.py:44
  42.0 30.8 %collective-permute-start.5 = (bf16[528,1280]{1,0:T(8,128)(2,1)S(1)}, bf16[528,1280]{1,0:T(8,128)(2,1)S(1)}, u32[]{:S(2)}, u32[]{:S(2)}) collective-permute-start(bf16[528,1280]{1,0:T(8,128)(2,1)S(1)} %assemble.1.refs_0_), channel_id=1, source_target_pairs={{0,16},{16,32},{32,48},{48,0},{1,17},{17,33},{33,49},{49,1},{2,18}... | collective-permute-start | bytes 4055048 | tf_op jit(solution)/shard_map/ppermute | solution.py:40
  42.3 33.1 %collective-permute-start.1 = (bf16[528,1280]{1,0:T(8,128)(2,1)S(1)}, bf16[528,1280]{1,0:T(8,128)(2,1)}, u32[]{:S(2)}, u32[]{:S(2)}) collective-permute-start(bf16[528,1280]{1,0:T(8,128)(2,1)S(1)} %assemble.1.refs_0_), channel_id=1, source_target_pairs={{0,64},{64,0},{1,65},{65,1},{2,66},{66,2},{3,67},{67,3},{4,68},{68... | collective-permute-start | bytes 4055048 | tf_op jit(solution)/shard_map/ppermute | solution.py:32
  72.7 16.6 %collective-permute-start.8 = (bf16[272,1280]{1,0:T(8,128)(2,1)S(1)}, bf16[272,1280]{1,0:T(8,128)(2,1)S(1)}, u32[]{:S(2)}, u32[]{:S(2)}) collective-permute-start(bf16[272,1280]{1,0:T(8,128)(2,1)S(1)} %slice.123), channel_id=1, source_target_pairs={{0,48},{16,0},{32,16},{48,32},{1,49},{17,1},{33,17},{49,33},{2,50}... | collective-permute-start | bytes 2088968 | tf_op jit(solution)/shard_map/ppermute | solution.py:44
  74.3 15.0 %collective-permute-start.7 = (bf16[256,1280]{1,0:T(8,128)(2,1)S(1)}, bf16[256,1280]{1,0:T(8,128)(2,1)}, u32[]{:S(2)}, u32[]{:S(2)}) collective-permute-start(bf16[256,1280]{1,0:T(8,128)(2,1)S(1)} %slice.122), channel_id=1, source_target_pairs={{0,16},{16,32},{32,48},{48,0},{1,17},{17,33},{33,49},{49,1},{2,18}... | collective-permute-start | bytes 1966088 | tf_op jit(solution)/shard_map/ppermute | solution.py:40
  75.4 11.8 %collective-permute-start.9 = (bf16[1024,256]{1,0:T(8,128)(2,1)S(1)}, bf16[1024,256]{1,0:T(8,128)(2,1)S(1)}, u32[]{:S(2)}, u32[]{:S(2)}) collective-permute-start(bf16[1024,256]{1,0:T(8,128)(2,1)S(1)} %copy-done.12), channel_id=1, source_target_pairs={{0,64},{64,0},{1,65},{65,1},{2,66},{66,2},{3,67},{67,3},{4,68},{68... | collective-permute-start | bytes 1572872 | tf_op jit(solution)/shard_map/ppermute | solution.py:32
  90.2 30.3 %collective-permute-start.10 = (bf16[528,1280]{1,0:T(8,128)(2,1)}, bf16[528,1280]{1,0:T(8,128)(2,1)S(1)}, u32[]{:S(2)}, u32[]{:S(2)}) collective-permute-start(bf16[528,1280]{1,0:T(8,128)(2,1)} %collective-permute-done.1.refs_3_), channel_id=1, source_target_pairs={{0,48},{16,0},{32,16},{48,32},{1,49},{17,1},{33,17},{49,33},{2,50}... | collective-permute-start | bytes 4055048 | tf_op jit(solution)/shard_map/ppermute | solution.py:44
  90.2 30.3 %collective-permute-start.11 = (bf16[528,1280]{1,0:T(8,128)(2,1)}, bf16[528,1280]{1,0:T(8,128)(2,1)}, u32[]{:S(2)}, u32[]{:S(2)}) collective-permute-start(bf16[528,1280]{1,0:T(8,128)(2,1)} %collective-permute-done.1.refs_3_), channel_id=1, source_target_pairs={{0,16},{16,32},{32,48},{48,0},{1,17},{17,33},{33,49},{49,1},{2,18}... | collective-permute-start | bytes 4055048 | tf_op jit(solution)/shard_map/ppermute | solution.py:40
  91.7 19.7 %collective-permute-start.12 = (bf16[256,1280]{1,0:T(8,128)(2,1)}, bf16[256,1280]{1,0:T(8,128)(2,1)}, u32[]{:S(2)}, u32[]{:S(2)}) collective-permute-start(bf16[256,1280]{1,0:T(8,128)(2,1)} %collective-permute-done.7.refs_4_), channel_id=1, source_target_pairs={{0,64},{64,0},{1,65},{65,1},{2,66},{66,2},{3,67},{67,3},{4,68},{68... | collective-permute-start | bytes 1966088 | tf_op jit(solution)/shard_map/ppermute | solution.py:32
  94.1 26.4 %collective-permute-start.13 = (bf16[272,1280]{1,0:T(8,128)(2,1)}, bf16[272,1280]{1,0:T(8,128)(2,1)S(1)}, u32[]{:S(2)}, u32[]{:S(2)}) collective-permute-start(bf16[272,1280]{1,0:T(8,128)(2,1)} %copy-done.10), channel_id=1, source_target_pairs={{0,64},{64,0},{1,65},{65,1},{2,66},{66,2},{3,67},{67,3},{4,68},{68... | collective-permute-start | bytes 2088968 | tf_op jit(solution)/shard_map/ppermute | solution.py:32
  129.6 10.3 %collective-permute-start.14 = (bf16[512,1408]{1,0:T(8,128)(2,1)}, bf16[512,1408]{1,0:T(8,128)(2,1)S(1)}, u32[]{:S(2)}, u32[]{:S(2)}) collective-permute-start(bf16[512,1408]{1,0:T(8,128)(2,1)} %get-tuple-element.26), channel_id=1, source_target_pairs={{0,8},{8,0},{1,9},{9,1},{2,10},{10,2},{3,11},{11,3},{4,12},{12,4},... | collective-permute-start | bytes 4325384 | tf_op jit(solution)/shard_map/ppermute | solution.py:32
  134.7 16.9 %collective-permute-start.17 = (bf16[1024,256]{1,0:T(8,128)(2,1)}, bf16[1024,256]{1,0:T(8,128)(2,1)S(1)}, u32[]{:S(2)}, u32[]{:S(2)}) collective-permute-start(bf16[1024,256]{1,0:T(8,128)(2,1)} %collective-permute-done.4.refs_4_), channel_id=1, source_target_pairs={{0,64},{64,0},{1,65},{65,1},{2,66},{66,2},{3,67},{67,3},{4,68},{68... | collective-permute-start | bytes 1572872 | tf_op jit(solution)/shard_map/ppermute | solution.py:32
  137.1 14.7 %collective-permute-start.15 = (bf16[1024,256]{1,0:T(8,128)(2,1)}, bf16[1024,256]{1,0:T(8,128)(2,1)S(1)}, u32[]{:S(2)}, u32[]{:S(2)}) collective-permute-start(bf16[1024,256]{1,0:T(8,128)(2,1)} %copy-done.14), channel_id=1, source_target_pairs={{0,16},{16,32},{32,48},{48,0},{1,17},{17,33},{33,49},{49,1},{2,18}... | collective-permute-start | bytes 1572872 | tf_op jit(solution)/shard_map/ppermute | solution.py:40
  137.1 14.7 %collective-permute-start.16 = (bf16[1024,256]{1,0:T(8,128)(2,1)}, bf16[1024,256]{1,0:T(8,128)(2,1)S(1)}, u32[]{:S(2)}, u32[]{:S(2)}) collective-permute-start(bf16[1024,256]{1,0:T(8,128)(2,1)} %copy-done.14), channel_id=1, source_target_pairs={{0,48},{16,0},{32,16},{48,32},{1,49},{17,1},{33,17},{49,33},{2,50}... | collective-permute-start | bytes 1572872 | tf_op jit(solution)/shard_map/ppermute | solution.py:44
  161.2 8.8 %collective-permute-start.24 = (bf16[256,512]{1,0:T(8,128)(2,1)S(1)}, bf16[256,512]{1,0:T(8,128)(2,1)S(1)}, u32[]{:S(2)}, u32[]{:S(2)}) collective-permute-start(bf16[256,512]{1,0:T(8,128)(2,1)S(1)} %get-tuple-element.36), channel_id=1, source_target_pairs={{0,1},{1,2},{2,3},{3,0},{4,5},{5,6},{6,7},{7,4},{8,9},{9,10},{10,1... | collective-permute-start | bytes 786440 | tf_op jit(solution)/shard_map/ppermute | solution.py:372
  161.6 8.3 %collective-permute-start.26 = (bf16[256,512]{1,0:T(8,128)(2,1)S(1)}, bf16[256,512]{1,0:T(8,128)(2,1)S(1)}, u32[]{:S(2)}, u32[]{:S(2)}) collective-permute-start(bf16[256,512]{1,0:T(8,128)(2,1)S(1)} %get-tuple-element.37), channel_id=1, source_target_pairs={{0,3},{1,0},{2,1},{3,2},{4,7},{5,4},{6,5},{7,6},{8,11},{9,8},{10,9... | collective-permute-start | bytes 786440 | tf_op jit(solution)/shard_map/ppermute | solution.py:373
  164.0 23.8 %collective-permute-start.19 = (bf16[8,64,1024]{2,1,0:T(8,128)(2,1)S(1)}, bf16[8,64,1024]{2,1,0:T(8,128)(2,1)S(1)}, u32[]{:S(2)}, u32[]{:S(2)}) collective-permute-start(bf16[8,64,1024]{2,1,0:T(8,128)(2,1)S(1)} %slice_bitcast_fusion), channel_id=1, source_target_pairs={{0,4},{4,0},{1,5},{5,1},{2,6},{6,2},{3,7},{7,3},{8,12},{12,8},{9,1... | collective-permute-start | bytes 3145736 | tf_op jit(solution)/shard_map/ppermute | solution.py:32
  170.2 13.5 %collective-permute-start.25 = (bf16[256,1024]{1,0:T(8,128)(2,1)S(1)}, bf16[256,1024]{1,0:T(8,128)(2,1)S(1)}, u32[]{:S(2)}, u32[]{:S(2)}) collective-permute-start(bf16[256,1024]{1,0:T(8,128)(2,1)S(1)} %pad_maximum_fusion), channel_id=1, source_target_pairs={{0,1},{1,2},{2,3},{3,0},{4,5},{5,6},{6,7},{7,4},{8,9},{9,10},{10,1... | collective-permute-start | bytes 1572872 | tf_op jit(solution)/shard_map/ppermute | solution.py:377
  170.3 13.3 %collective-permute-start.27 = (bf16[256,1024]{1,0:T(8,128)(2,1)S(1)}, bf16[256,1024]{1,0:T(8,128)(2,1)S(1)}, u32[]{:S(2)}, u32[]{:S(2)}) collective-permute-start(bf16[256,1024]{1,0:T(8,128)(2,1)S(1)} %pad_maximum_fusion.1), channel_id=1, source_target_pairs={{0,3},{1,0},{2,1},{3,2},{4,7},{5,4},{6,5},{7,6},{8,11},{9,8},{10,9... | collective-permute-start | bytes 1572872 | tf_op jit(solution)/shard_map/ppermute | solution.py:378
  (32 other events, 265.1 us)

commit v2 on v1

--- a/solution.py
+++ b/solution.py
@@ -70,7 +70,7 @@
     return pl.pallas_call(
         deal_kernel,
         out_shape=jax.ShapeDtypeStruct((16 * groups.shape[0], WIDTH + 128), BF16),
-        compiler_params=pltpu.CompilerParams(vmem_limit_bytes=16 * 1024 * 1024),
+        compiler_params=pltpu.CompilerParams(vmem_limit_bytes=60 * 1024 * 1024),
         name="deal",
     )(groups, inputs, gates, steps)
 
@@ -328,7 +328,7 @@
             out_specs=pl.BlockSpec((rows, 2 * width), lambda i, _: (0, 0)),
         ),
         out_shape=jax.ShapeDtypeStruct((rows, 2 * width), BF16),
-        compiler_params=pltpu.CompilerParams(vmem_limit_bytes=FAST),
+        compiler_params=pltpu.CompilerParams(vmem_limit_bytes=4 * 1024 * 1024),
         name="place",
     )(table, kept, given)
 
@@ -421,9 +421,10 @@
 
     half = KB // 2
     w_r, w_l = right(w_out), left(w_out)
-    w_f = lax.ppermute(w_out, "x", ring(4, 2))
-    s_r, s_l, s_o = right(s_own, w_r, w_l, w_f), left(s_own, w_r, w_l, w_f), over(s_own)
-    w_o = over(w_out, s_o)
+    w_ft, w_fb = right(w_r[:KB]), left(w_l[KB:])
+    w_f = jnp.concatenate([w_ft, w_fb], axis=0)
+    s_r, s_l, s_o = right(s_own, w_r, w_l), left(s_own, w_r, w_l), over(s_own, w_ft, w_fb)
+    w_o = over(w_out, s_o, w_f)
     s_ft, s_fb = right(s_r[:half], s_l), left(s_l[half:], s_r)
     near = project_part(
         hidden_in,

time: 208 us -> 200 us (0.962)
  waiting for transfers between devices: 100 us -> 91.8 us
  starting transfers between devices: 52.1 us -> 54.7 us
  local copies, waits for them, and re-layouts: 12.8 us -> 10.7 us
    all_to_all x1, waiting for transfers between devices: 16.2 us -> 1.43 us  [shards(): s_own = assemble(lax.all_to_all(blocks, group, 0, 0, tiled=True))]
    ppermute x5 -> x6, waiting for transfers between devices: 3.74 us -> 15.4 us  [right(): return lax.ppermute(after(value, *others), 'x', ring(4, 1))]
    ppermute x5 -> x6, starting transfers between devices: 5.69 us -> 12.4 us  [left(): return lax.ppermute(after(value, *others), 'x', ring(4, -1))]
    ppermute x1 -> x0, waiting for transfers between devices: 6.45 us -> none  [shards(): w_f = lax.ppermute(w_out, 'x', ring(4, 2))]
    unnamed x52 -> x57, local copies, waits for them, and re-layouts: 12 us -> 7.41 us
    ppermute x5 -> x6, starting transfers between devices: 4.15 us -> 1.69 us  [right(): return lax.ppermute(after(value, *others), 'x', ring(4, 1))]
    ppermute x5 -> x6, waiting for transfers between devices: 26.3 us -> 26.1 us  [left(): return lax.ppermute(after(value, *others), 'x', ring(4, -1))]
  transfers between devices with their start and end apart: 31 -> 32, of which waited for: 15 -> 15; matrix products, arithmetic and copies ran while one was open for 1% -> 2% of each run, Pallas kernels for 12% -> 13%
where the time goes in v2:
time: 200 us; the launch traced here: 199 us
  waiting for transfers between devices  91.8 us (46%)
  starting transfers between devices  54.7 us (27%)
  Pallas kernels  39.5 us (20%)
  local copies, waits for them, and re-layouts  10.7 us (5%)
    ppermute x11, waiting for transfers between devices, swap(): return lax.ppermute(value, axis, [(0, 1), (1, 0)])  27.1 us
    ppermute x6, waiting for transfers between devices, left(): return lax.ppermute(after(value, *others), 'x', ring(4, -1))  26.1 us
    ppermute x11, starting transfers between devices, swap(): return lax.ppermute(value, axis, [(0, 1), (1, 0)])  22.6 us
    pallas_call x2, Pallas kernels, project_part(): pl.pallas_call(functools.partial(project_kernel, steps, counts, bool(sums...  20.7 us
    ppermute x6, waiting for transfers between devices, right(): return lax.ppermute(after(value, *others), 'x', ring(4, 1))  15.4 us
    ppermute x2, waiting for transfers between devices, reduce_z(): from_below = lax.ppermute(up, 'z', ring(4, 1))  14 us
    ppermute x6, starting transfers between devices, left(): return lax.ppermute(after(value, *others), 'x', ring(4, -1))  12.4 us
    pallas_call x1, Pallas kernels, scan(): pl.pallas_call(scan_kernel, grid_spec=pltpu.PrefetchScalarGridSpec(num_sc...  10.3 us
  transfers between devices with their start and end apart: 32, of which 15 were waited for; matrix products, arithmetic and copies ran while one was open for 2% of the time, Pallas kernels for 13%

profile of v2, /device:TPU:1, one launch (start us, length us, event | category | flops | bytes accessed | tf_op | source)
XLA Modules:
  0.0 199.2 jit_solution(4221443544287196186)
XLA Ops:
  2.1 2.5 %deal.1 = bf16[512,1408]{1,0:T(8,128)(2,1)} custom-call(bf16[32,4096]{1,0:T(8,128)(2,1)} %groups_ref.1, bf16[32,8192]{1,0:T(8,128)(2,1)} %input_ref.1, bf16[32,8192]{1,0:T(8,128)(2,1)} %gate_ref.1, bf16[32,128]{1,0:T(8,128)(2,1)} %step_ref.1), custom_call_target="tpu_custom_call" | custom-call | tf_op jit(solution)/shard_map/deal/pallas_call | solution.py:70
  4.6 6.7 %all-to-all-start = ((bf16[16,32,1408]{2,1,0:T(8,128)(2,1)}), bf16[16,32,1408]{2,1,0:T(8,128)(2,1)S(1)}, u32[]{:S(2)}, u32[]{:S(2)}) async-start(bf16[16,32,1408]{2,1,0:T(8,128)(2,1)} %bitcast.69), calls=%async_computation | async-start | bytes 2883584 | tf_op jit(solution)/shard_map/all_to_all | solution.py:419
  14.1 12.0 %collective-permute-done.1.refs_2_ = bf16[1024,256]{1,0:T(8,128)(2,1)S(1)} collective-permute-done((bf16[1024,256]{1,0:T(8,128)(2,1)S(1)}, bf16[1024,256]{1,0:T(8,128)(2,1)S(1)}, u32[]{:S(2)}, u32[]{:S(2)}) %collective-permute-start.1) | collective-permute-done | bytes 524320 | tf_op jit(solution)/shard_map/ppermute | solution.py:40
  27.7 2.7 %collective-permute-start.4 = (bf16[512,256]{1,0:T(8,128)(2,1)}, bf16[512,256]{1,0:T(8,128)(2,1)}, u32[]{:S(2)}, u32[]{:S(2)}) collective-permute-start(bf16[512,256]{1,0:T(8,128)(2,1)} %slice.131), channel_id=1, source_target_pairs={{0,48},{16,0},{32,16},{48,32},{1,49},{17,1},{33,17},{49,33},{2,50}... | collective-permute-start | bytes 786440 | tf_op jit(solution)/shard_map/ppermute | solution.py:44
  31.9 2.5 %collective-permute-start.7 = (bf16[528,1280]{1,0:T(8,128)(2,1)S(1)}, bf16[528,1280]{1,0:T(8,128)(2,1)S(1)}, u32[]{:S(2)}, u32[]{:S(2)}) collective-permute-start(bf16[528,1280]{1,0:T(8,128)(2,1)S(1)} %assemble.1.refs_0_), channel_id=1, source_target_pairs={{0,48},{16,0},{32,16},{48,32},{1,49},{17,1},{33,17},{49,33},{2,50}... | collective-permute-start | bytes 4055048 | tf_op jit(solution)/shard_map/ppermute | solution.py:44
  35.3 2.6 %collective-permute-start.5 = (bf16[528,1280]{1,0:T(8,128)(2,1)S(1)}, bf16[528,1280]{1,0:T(8,128)(2,1)}, u32[]{:S(2)}, u32[]{:S(2)}) collective-permute-start(bf16[528,1280]{1,0:T(8,128)(2,1)S(1)} %assemble.1.refs_0_), channel_id=1, source_target_pairs={{0,64},{64,0},{1,65},{65,1},{2,66},{66,2},{3,67},{67,3},{4,68},{68... | collective-permute-start | bytes 4055048 | tf_op jit(solution)/shard_map/ppermute | solution.py:32
  37.9 26.1 %collective-permute-done.7.refs_1_ = bf16[528,1280]{1,0:T(8,128)(2,1)S(1)} collective-permute-done((bf16[528,1280]{1,0:T(8,128)(2,1)S(1)}, bf16[528,1280]{1,0:T(8,128)(2,1)S(1)}, u32[]{:S(2)}, u32[]{:S(2)}) %collective-permute-start.7) | collective-permute-done | bytes 1351712 | tf_op jit(solution)/shard_map/ppermute | solution.py:44
  70.1 2.6 %collective-permute-start.10 = (bf16[1024,256]{1,0:T(8,128)(2,1)S(1)}, bf16[1024,256]{1,0:T(8,128)(2,1)S(1)}, u32[]{:S(2)}, u32[]{:S(2)}) collective-permute-start(bf16[1024,256]{1,0:T(8,128)(2,1)S(1)} %copy-done.14), channel_id=1, source_target_pairs={{0,64},{64,0},{1,65},{65,1},{2,66},{66,2},{3,67},{67,3},{4,68},{68... | collective-permute-start | bytes 1572872 | tf_op jit(solution)/shard_map/ppermute | solution.py:32
  72.7 10.4 %collective-permute-done.10.refs_3_ = bf16[1024,256]{1,0:T(8,128)(2,1)S(1)} collective-permute-done((bf16[1024,256]{1,0:T(8,128)(2,1)S(1)}, bf16[1024,256]{1,0:T(8,128)(2,1)S(1)}, u32[]{:S(2)}, u32[]{:S(2)}) %collective-permute-start.10) | collective-permute-done | bytes 524320 | tf_op jit(solution)/shard_map/ppermute | solution.py:32
  92.1 12.8 %project.2 = (f32[512,1408]{1,0:T(8,128)}, f32[512,1408]{1,0:T(8,128)}) custom-call(s32[5]{0:T(128)S(1)} %stack.107.table, bf16[512,4096]{1,0:T(8,128)(2,1)} %own_hbm.3, bf16[512,4096]{1,0:T(8,128)(2,1)} %collective-permute-done.oth_hbm, bf16[528,1280]{1,0:T(8,128)(2,1)S(1)} %assemble.1.refs_0_, bf16[528,1280]{1,0:T(8,128)(2,1)S(1)} %copy-done.1, ...), custom_call_target="tpu_custom_call" | custom-call | flops 6710886400 | bytes 19660800 | tf_op jit(solution)/shard_map/project/pallas_call | solution.py:164
  104.9 9.4 %collective-permute-done.14.refs_3_ = bf16[272,1280]{1,0:T(8,128)(2,1)S(1)} collective-permute-done((bf16[272,1280]{1,0:T(8,128)(2,1)}, bf16[272,1280]{1,0:T(8,128)(2,1)S(1)}, u32[]{:S(2)}, u32[]{:S(2)}) %collective-permute-start.14) | collective-permute-done | bytes 696352 | tf_op jit(solution)/shard_map/ppermute | solution.py:32
  114.4 7.8 %project.3 = (bf16[512,1408]{1,0:T(8,128)(2,1)S(1)}, bf16[512,1408]{1,0:T(8,128)(2,1)}) custom-call(s32[3]{0:T(128)S(1)} %pad_add_fusion.1.table, bf16[512,4096]{1,0:T(8,128)(2,1)} %own_hbm.3, bf16[512,4096]{1,0:T(8,128)(2,1)} %collective-permute-done.oth_hbm, bf16[528,1280]{1,0:T(8,128)(2,1)S(1)} %collective-permute-done.11.refs_0_, ...), custom_call_target="tpu_custom_call" | custom-call | flops 4026531840 | bytes 14942208 | tf_op jit(solution)/shard_map/project/pallas_call | solution.py:164
  123.4 4.6 %collective-permute-start.15 = (bf16[512,1408]{1,0:T(8,128)(2,1)}, bf16[512,1408]{1,0:T(8,128)(2,1)S(1)}, u32[]{:S(2)}, u32[]{:S(2)}) collective-permute-start(bf16[512,1408]{1,0:T(8,128)(2,1)} %get-tuple-element.28), channel_id=1, source_target_pairs={{0,8},{8,0},{1,9},{9,1},{2,10},{10,2},{3,11},{11,3},{4,12},{12,4},... | collective-permute-start | bytes 4325384 | tf_op jit(solution)/shard_map/ppermute | solution.py:32
  130.6 2.7 %collective-permute-start.17 = (bf16[1024,256]{1,0:T(8,128)(2,1)}, bf16[1024,256]{1,0:T(8,128)(2,1)S(1)}, u32[]{:S(2)}, u32[]{:S(2)}) collective-permute-start(bf16[1024,256]{1,0:T(8,128)(2,1)} %copy-done.16), channel_id=1, source_target_pairs={{0,48},{16,0},{32,16},{48,32},{1,49},{17,1},{33,17},{49,33},{2,50}... | collective-permute-start | bytes 1572872 | tf_op jit(solution)/shard_map/ppermute | solution.py:44
  134.8 10.3 %scan.1 = (bf16[512,1024]{1,0:T(8,128)(2,1)S(1)}, f32[4,16,64,256]{3,2,1,0:T(8,128)}) custom-call(s32[13]{0:T(128)S(1)} %pad_add_fusion.info, bf16[512,1408]{1,0:T(8,128)(2,1)S(1)} %copy-done.11, bf16[512,1408]{1,0:T(8,128)(2,1)S(1)} %collective-permute-done.15.got, bf16[4,3,1024]{2,1,0:T(4,128)(2,1)S(1)} %copy.21.tail_x, ...), custom_call_target="tpu_custom_call" | custom-call | flops 2000000000 | bytes 14000000 | tf_op jit(solution)/shard_map/scan/pallas_call | solution.py:279
  148.7 4.5 %multiply.1 = (bf16[1024,1024]{1,0:T(8,128)(2,1)S(1)}, bf16[1024,1024]{1,0:T(8,128)(2,1)S(1)}) custom-call(bf16[512,1024]{1,0:T(8,128)(2,1)S(1)} %get-tuple-element.32.own_ref, bf16[512,1024]{1,0:T(8,128)(2,1)S(1)} %collective-permute-done.19.oth_ref, bf16[1024,256]{1,0:T(8,128)(2,1)S(1)} %copy-done.15, bf16[1024,256]{1,0:T(8,128)(2,1)S(1)} %copy-done.7, ...), custom_call_target="tpu_custom_call" | custom-call | flops 4294967296 | bytes 10485760 | tf_op jit(solution)/shard_map/multiply/pallas_call | solution.py:353
  156.3 5.8 %collective-permute-done.25 = bf16[256,512]{1,0:T(8,128)(2,1)S(1)} collective-permute-done((bf16[256,512]{1,0:T(8,128)(2,1)S(1)}, bf16[256,512]{1,0:T(8,128)(2,1)S(1)}, u32[]{:S(2)}, u32[]{:S(2)}) %collective-permute-start.25) | collective-permute-done | bytes 262176 | tf_op jit(solution)/shard_map/ppermute | solution.py:372
  162.5 2.7 %collective-permute-start.28 = (bf16[256,1024]{1,0:T(8,128)(2,1)S(1)}, bf16[256,1024]{1,0:T(8,128)(2,1)S(1)}, u32[]{:S(2)}, u32[]{:S(2)}) collective-permute-start(bf16[256,1024]{1,0:T(8,128)(2,1)S(1)} %pad_maximum_fusion.1), channel_id=1, source_target_pairs={{0,3},{1,0},{2,1},{3,2},{4,7},{5,4},{6,5},{7,6},{8,11},{9,8},{10,9... | collective-permute-start | bytes 1572872 | tf_op jit(solution)/shard_map/ppermute | solution.py:378
  165.2 10.6 %collective-permute-done.26 = bf16[256,1024]{1,0:T(8,128)(2,1)S(1)} collective-permute-done((bf16[256,1024]{1,0:T(8,128)(2,1)S(1)}, bf16[256,1024]{1,0:T(8,128)(2,1)S(1)}, u32[]{:S(2)}, u32[]{:S(2)}) %collective-permute-start.26) | collective-permute-done | bytes 524320 | tf_op jit(solution)/shard_map/ppermute | solution.py:377
  176.1 3.9 %collective-permute-done.20 = bf16[8,64,1024]{2,1,0:T(8,128)(2,1)S(1)} collective-permute-done((bf16[8,64,1024]{2,1,0:T(8,128)(2,1)S(1)}, bf16[8,64,1024]{2,1,0:T(8,128)(2,1)S(1)}, u32[]{:S(2)}, u32[]{:S(2)}) %collective-permute-start.20) | collective-permute-done | bytes 1048608 | tf_op jit(solution)/shard_map/ppermute | solution.py:32
  180.9 2.7 %collective-permute-start.23 = (bf16[128,512]{1,0:T(8,128)(2,1)S(1)}, bf16[128,512]{1,0:T(8,128)(2,1)S(1)}, u32[]{:S(2)}, u32[]{:S(2)}) collective-permute-start(bf16[128,512]{1,0:T(8,128)(2,1)S(1)} %get-tuple-element.49), channel_id=1, source_target_pairs={{0,3},{1,0},{2,1},{3,2},{4,7},{5,4},{6,5},{7,6},{8,11},{9,8},{10,9... | collective-permute-start | bytes 393224 | tf_op jit(solution)/shard_map/ppermute | solution.py:373
  185.8 2.9 %collective-permute-start.24 = (bf16[128,1024]{1,0:T(8,128)(2,1)S(1)}, bf16[128,1024]{1,0:T(8,128)(2,1)S(1)}, u32[]{:S(2)}, u32[]{:S(2)}) collective-permute-start(bf16[128,1024]{1,0:T(8,128)(2,1)S(1)} %pad_maximum_fusion.4), channel_id=1, source_target_pairs={{0,3},{1,0},{2,1},{3,2},{4,7},{5,4},{6,5},{7,6},{8,11},{9,8},{10,9... | collective-permute-start | bytes 786440 | tf_op jit(solution)/shard_map/ppermute | solution.py:378
  188.8 3.4 %collective-permute-done.22 = bf16[128,1024]{1,0:T(8,128)(2,1)S(1)} collective-permute-done((bf16[128,1024]{1,0:T(8,128)(2,1)S(1)}, bf16[128,1024]{1,0:T(8,128)(2,1)S(1)}, u32[]{:S(2)}, u32[]{:S(2)}) %collective-permute-start.22) | collective-permute-done | bytes 262176 | tf_op jit(solution)/shard_map/ppermute | solution.py:377
  192.4 4.3 %collective-permute-start.30 = (bf16[64,2048]{1,0:T(8,128)(2,1)S(1)}, bf16[64,2048]{1,0:T(8,128)(2,1)S(1)}, u32[]{:S(2)}, u32[]{:S(2)}) collective-permute-start(bf16[64,2048]{1,0:T(8,128)(2,1)S(1)} %get-tuple-element.46), channel_id=1, source_target_pairs={{0,8},{8,0},{1,9},{9,1},{2,10},{10,2},{3,11},{11,3},{4,12},{12,4},... | collective-permute-start | bytes 786440 | tf_op jit(solution)/shard_map/ppermute | solution.py:32
  (136 shorter events, 41.5 us)
Async XLA Ops:
  0.6 87.7 %collective-permute-start = (bf16[512,4096]{1,0:T(8,128)(2,1)}, bf16[512,4096]{1,0:T(8,128)(2,1)}, u32[]{:S(2)}, u32[]{:S(2)}) collective-permute-start(bf16[512,4096]{1,0:T(8,128)(2,1)} %own_hbm.3), channel_id=1, source_target_pairs={{0,8},{8,0},{1,9},{9,1},{2,10},{10,2},{3,11},{11,3},{4,12},{12,4},... | collective-permute-start | bytes 12582920 | tf_op jit(solution)/shard_map/ppermute | solution.py:32
  4.6 27.2 %all-to-all-start = ((bf16[16,32,1408]{2,1,0:T(8,128)(2,1)}), bf16[16,32,1408]{2,1,0:T(8,128)(2,1)S(1)}, u32[]{:S(2)}, u32[]{:S(2)}) async-start(bf16[16,32,1408]{2,1,0:T(8,128)(2,1)} %bitcast.69), calls=%async_computation | async-start | bytes 2883584 | tf_op jit(solution)/shard_map/all_to_all | solution.py:419
  11.3 14.8 %collective-permute-start.1 = (bf16[1024,256]{1,0:T(8,128)(2,1)S(1)}, bf16[1024,256]{1,0:T(8,128)(2,1)S(1)}, u32[]{:S(2)}, u32[]{:S(2)}) collective-permute-start(bf16[1024,256]{1,0:T(8,128)(2,1)S(1)} %copy-done.14), channel_id=1, source_target_pairs={{0,16},{16,32},{32,48},{48,0},{1,17},{17,33},{33,49},{49,1},{2,18}... | collective-permute-start | bytes 1572872 | tf_op jit(solution)/shard_map/ppermute | solution.py:40
  12.6 14.2 %collective-permute-start.3 = (bf16[1024,256]{1,0:T(8,128)(2,1)S(1)}, bf16[1024,256]{1,0:T(8,128)(2,1)S(1)}, u32[]{:S(2)}, u32[]{:S(2)}) collective-permute-start(bf16[1024,256]{1,0:T(8,128)(2,1)S(1)} %copy-done.14), channel_id=1, source_target_pairs={{0,48},{16,0},{32,16},{48,32},{1,49},{17,1},{33,17},{49,33},{2,50}... | collective-permute-start | bytes 1572872 | tf_op jit(solution)/shard_map/ppermute | solution.py:44
  26.8 8.5 %collective-permute-start.2 = (bf16[512,256]{1,0:T(8,128)(2,1)}, bf16[512,256]{1,0:T(8,128)(2,1)}, u32[]{:S(2)}, u32[]{:S(2)}) collective-permute-start(bf16[512,256]{1,0:T(8,128)(2,1)} %slice.130), channel_id=1, source_target_pairs={{0,16},{16,32},{32,48},{48,0},{1,17},{17,33},{33,49},{49,1},{2,18}... | collective-permute-start | bytes 786440 | tf_op jit(solution)/shard_map/ppermute | solution.py:40
  31.9 32.1 %collective-permute-start.7 = (bf16[528,1280]{1,0:T(8,128)(2,1)S(1)}, bf16[528,1280]{1,0:T(8,128)(2,1)S(1)}, u32[]{:S(2)}, u32[]{:S(2)}) collective-permute-start(bf16[528,1280]{1,0:T(8,128)(2,1)S(1)} %assemble.1.refs_0_), channel_id=1, source_target_pairs={{0,48},{16,0},{32,16},{48,32},{1,49},{17,1},{33,17},{49,33},{2,50}... | collective-permute-start | bytes 4055048 | tf_op jit(solution)/shard_map/ppermute | solution.py:44
  34.5 32.0 %collective-permute-start.6 = (bf16[528,1280]{1,0:T(8,128)(2,1)S(1)}, bf16[528,1280]{1,0:T(8,128)(2,1)S(1)}, u32[]{:S(2)}, u32[]{:S(2)}) collective-permute-start(bf16[528,1280]{1,0:T(8,128)(2,1)S(1)} %assemble.1.refs_0_), channel_id=1, source_target_pairs={{0,16},{16,32},{32,48},{48,0},{1,17},{17,33},{33,49},{49,1},{2,18}... | collective-permute-start | bytes 4055048 | tf_op jit(solution)/shard_map/ppermute | solution.py:40
  35.3 34.7 %collective-permute-start.5 = (bf16[528,1280]{1,0:T(8,128)(2,1)S(1)}, bf16[528,1280]{1,0:T(8,128)(2,1)}, u32[]{:S(2)}, u32[]{:S(2)}) collective-permute-start(bf16[528,1280]{1,0:T(8,128)(2,1)S(1)} %assemble.1.refs_0_), channel_id=1, source_target_pairs={{0,64},{64,0},{1,65},{65,1},{2,66},{66,2},{3,67},{67,3},{4,68},{68... | collective-permute-start | bytes 4055048 | tf_op jit(solution)/shard_map/ppermute | solution.py:32
  66.5 16.6 %collective-permute-start.9 = (bf16[272,1280]{1,0:T(8,128)(2,1)S(1)}, bf16[272,1280]{1,0:T(8,128)(2,1)S(1)}, u32[]{:S(2)}, u32[]{:S(2)}) collective-permute-start(bf16[272,1280]{1,0:T(8,128)(2,1)S(1)} %slice.133), channel_id=1, source_target_pairs={{0,48},{16,0},{32,16},{48,32},{1,49},{17,1},{33,17},{49,33},{2,50}... | collective-permute-start | bytes 2088968 | tf_op jit(solution)/shard_map/ppermute | solution.py:44
  67.7 15.4 %collective-permute-start.8 = (bf16[256,1280]{1,0:T(8,128)(2,1)S(1)}, bf16[256,1280]{1,0:T(8,128)(2,1)}, u32[]{:S(2)}, u32[]{:S(2)}) collective-permute-start(bf16[256,1280]{1,0:T(8,128)(2,1)S(1)} %slice.132), channel_id=1, source_target_pairs={{0,16},{16,32},{32,48},{48,0},{1,17},{17,33},{33,49},{49,1},{2,18}... | collective-permute-start | bytes 1966088 | tf_op jit(solution)/shard_map/ppermute | solution.py:40
  70.1 13.0 %collective-permute-start.10 = (bf16[1024,256]{1,0:T(8,128)(2,1)S(1)}, bf16[1024,256]{1,0:T(8,128)(2,1)S(1)}, u32[]{:S(2)}, u32[]{:S(2)}) collective-permute-start(bf16[1024,256]{1,0:T(8,128)(2,1)S(1)} %copy-done.14), channel_id=1, source_target_pairs={{0,64},{64,0},{1,65},{65,1},{2,66},{66,2},{3,67},{67,3},{4,68},{68... | collective-permute-start | bytes 1572872 | tf_op jit(solution)/shard_map/ppermute | solution.py:32
  83.1 31.2 %collective-permute-start.11 = (bf16[528,1280]{1,0:T(8,128)(2,1)}, bf16[528,1280]{1,0:T(8,128)(2,1)S(1)}, u32[]{:S(2)}, u32[]{:S(2)}) collective-permute-start(bf16[528,1280]{1,0:T(8,128)(2,1)} %collective-permute-done.5.refs_3_), channel_id=1, source_target_pairs={{0,48},{16,0},{32,16},{48,32},{1,49},{17,1},{33,17},{49,33},{2,50}... | collective-permute-start | bytes 4055048 | tf_op jit(solution)/shard_map/ppermute | solution.py:44
  85.0 29.3 %collective-permute-start.12 = (bf16[528,1280]{1,0:T(8,128)(2,1)}, bf16[528,1280]{1,0:T(8,128)(2,1)}, u32[]{:S(2)}, u32[]{:S(2)}) collective-permute-start(bf16[528,1280]{1,0:T(8,128)(2,1)} %collective-permute-done.5.refs_3_), channel_id=1, source_target_pairs={{0,16},{16,32},{32,48},{48,0},{1,17},{17,33},{33,49},{49,1},{2,18}... | collective-permute-start | bytes 4055048 | tf_op jit(solution)/shard_map/ppermute | solution.py:40
  85.1 19.8 %collective-permute-start.13 = (bf16[256,1280]{1,0:T(8,128)(2,1)}, bf16[256,1280]{1,0:T(8,128)(2,1)}, u32[]{:S(2)}, u32[]{:S(2)}) collective-permute-start(bf16[256,1280]{1,0:T(8,128)(2,1)} %collective-permute-done.8.refs_4_), channel_id=1, source_target_pairs={{0,64},{64,0},{1,65},{65,1},{2,66},{66,2},{3,67},{67,3},{4,68},{68... | collective-permute-start | bytes 1966088 | tf_op jit(solution)/shard_map/ppermute | solution.py:32
  87.6 26.7 %collective-permute-start.14 = (bf16[272,1280]{1,0:T(8,128)(2,1)}, bf16[272,1280]{1,0:T(8,128)(2,1)S(1)}, u32[]{:S(2)}, u32[]{:S(2)}) collective-permute-start(bf16[272,1280]{1,0:T(8,128)(2,1)} %copy-done.12), channel_id=1, source_target_pairs={{0,64},{64,0},{1,65},{65,1},{2,66},{66,2},{3,67},{67,3},{4,68},{68... | collective-permute-start | bytes 2088968 | tf_op jit(solution)/shard_map/ppermute | solution.py:32
  123.4 10.1 %collective-permute-start.15 = (bf16[512,1408]{1,0:T(8,128)(2,1)}, bf16[512,1408]{1,0:T(8,128)(2,1)S(1)}, u32[]{:S(2)}, u32[]{:S(2)}) collective-permute-start(bf16[512,1408]{1,0:T(8,128)(2,1)} %get-tuple-element.28), channel_id=1, source_target_pairs={{0,8},{8,0},{1,9},{9,1},{2,10},{10,2},{3,11},{11,3},{4,12},{12,4},... | collective-permute-start | bytes 4325384 | tf_op jit(solution)/shard_map/ppermute | solution.py:32
  128.2 17.0 %collective-permute-start.18 = (bf16[1024,256]{1,0:T(8,128)(2,1)S(1)}, bf16[1024,256]{1,0:T(8,128)(2,1)S(1)}, u32[]{:S(2)}, u32[]{:S(2)}) collective-permute-start(bf16[1024,256]{1,0:T(8,128)(2,1)S(1)} %copy-done.9), channel_id=1, source_target_pairs={{0,64},{64,0},{1,65},{65,1},{2,66},{66,2},{3,67},{67,3},{4,68},{68... | collective-permute-start | bytes 1572872 | tf_op jit(solution)/shard_map/ppermute | solution.py:32
  130.6 14.7 %collective-permute-start.16 = (bf16[1024,256]{1,0:T(8,128)(2,1)}, bf16[1024,256]{1,0:T(8,128)(2,1)S(1)}, u32[]{:S(2)}, u32[]{:S(2)}) collective-permute-start(bf16[1024,256]{1,0:T(8,128)(2,1)} %copy-done.16), channel_id=1, source_target_pairs={{0,16},{16,32},{32,48},{48,0},{1,17},{17,33},{33,49},{49,1},{2,18}... | collective-permute-start | bytes 1572872 | tf_op jit(solution)/shard_map/ppermute | solution.py:40
  130.6 14.7 %collective-permute-start.17 = (bf16[1024,256]{1,0:T(8,128)(2,1)}, bf16[1024,256]{1,0:T(8,128)(2,1)S(1)}, u32[]{:S(2)}, u32[]{:S(2)}) collective-permute-start(bf16[1024,256]{1,0:T(8,128)(2,1)} %copy-done.16), channel_id=1, source_target_pairs={{0,48},{16,0},{32,16},{48,32},{1,49},{17,1},{33,17},{49,33},{2,50}... | collective-permute-start | bytes 1572872 | tf_op jit(solution)/shard_map/ppermute | solution.py:44
  153.3 8.8 %collective-permute-start.25 = (bf16[256,512]{1,0:T(8,128)(2,1)S(1)}, bf16[256,512]{1,0:T(8,128)(2,1)S(1)}, u32[]{:S(2)}, u32[]{:S(2)}) collective-permute-start(bf16[256,512]{1,0:T(8,128)(2,1)S(1)} %get-tuple-element.38), channel_id=1, source_target_pairs={{0,1},{1,2},{2,3},{3,0},{4,5},{5,6},{6,7},{7,4},{8,9},{9,10},{10,1... | collective-permute-start | bytes 786440 | tf_op jit(solution)/shard_map/ppermute | solution.py:372
  153.8 8.3 %collective-permute-start.27 = (bf16[256,512]{1,0:T(8,128)(2,1)S(1)}, bf16[256,512]{1,0:T(8,128)(2,1)S(1)}, u32[]{:S(2)}, u32[]{:S(2)}) collective-permute-start(bf16[256,512]{1,0:T(8,128)(2,1)S(1)} %get-tuple-element.39), channel_id=1, source_target_pairs={{0,3},{1,0},{2,1},{3,2},{4,7},{5,4},{6,5},{7,6},{8,11},{9,8},{10,9... | collective-permute-start | bytes 786440 | tf_op jit(solution)/shard_map/ppermute | solution.py:373
  156.2 23.8 %collective-permute-start.20 = (bf16[8,64,1024]{2,1,0:T(8,128)(2,1)S(1)}, bf16[8,64,1024]{2,1,0:T(8,128)(2,1)S(1)}, u32[]{:S(2)}, u32[]{:S(2)}) collective-permute-start(bf16[8,64,1024]{2,1,0:T(8,128)(2,1)S(1)} %slice_bitcast_fusion), channel_id=1, source_target_pairs={{0,4},{4,0},{1,5},{5,1},{2,6},{6,2},{3,7},{7,3},{8,12},{12,8},{9,1... | collective-permute-start | bytes 3145736 | tf_op jit(solution)/shard_map/ppermute | solution.py:32
  162.3 13.5 %collective-permute-start.26 = (bf16[256,1024]{1,0:T(8,128)(2,1)S(1)}, bf16[256,1024]{1,0:T(8,128)(2,1)S(1)}, u32[]{:S(2)}, u32[]{:S(2)}) collective-permute-start(bf16[256,1024]{1,0:T(8,128)(2,1)S(1)} %pad_maximum_fusion), channel_id=1, source_target_pairs={{0,1},{1,2},{2,3},{3,0},{4,5},{5,6},{6,7},{7,4},{8,9},{9,10},{10,1... | collective-permute-start | bytes 1572872 | tf_op jit(solution)/shard_map/ppermute | solution.py:377
  162.5 13.3 %collective-permute-start.28 = (bf16[256,1024]{1,0:T(8,128)(2,1)S(1)}, bf16[256,1024]{1,0:T(8,128)(2,1)S(1)}, u32[]{:S(2)}, u32[]{:S(2)}) collective-permute-start(bf16[256,1024]{1,0:T(8,128)(2,1)S(1)} %pad_maximum_fusion.1), channel_id=1, source_target_pairs={{0,3},{1,0},{2,1},{3,2},{4,7},{5,4},{6,5},{7,6},{8,11},{9,8},{10,9... | collective-permute-start | bytes 1572872 | tf_op jit(solution)/shard_map/ppermute | solution.py:378
  (35 other events, 342.0 us)

commit v3 on v2

--- a/solution.py
+++ b/solution.py
@@ -226,8 +226,15 @@
     raw = own_v[:, WIDTH:] + got_v[:, WIDTH:] + bias[...]
     step = jnp.maximum(raw, 0.0) + jnp.log1p(jnp.exp(-jnp.abs(raw)))
     step = jnp.where((rows < live_to) & (cols < HEADS), step, 0.0)
-    lower = (rows >= cols).astype(F32)
-    total = jnp.dot(lower, -rate[...] * step, precision=lax.Precision.HIGHEST, preferred_element_type=F32)
+    lower = (rows >= cols).astype(F32).astype(BF16)
+    left_over = -rate[...] * step
+    pieces = []
+    for _ in range(3):
+        pieces.append(left_over.astype(BF16))
+        left_over = left_over - pieces[-1].astype(F32)
+    total = jnp.dot(
+        jnp.concatenate([lower] * 3, axis=1), jnp.concatenate(pieces, axis=0), preferred_element_type=F32
+    )
     step_t = step.T
     total_t = total.T
     end_t = total_t[:, LEN - 1 : LEN]

time: 200 us -> 200 us (level)
  no operation moved by 1% of the time
where the time goes in v3:
time: 200 us; the launch traced here: 199 us
  waiting for transfers between devices  92.3 us (46%)
  starting transfers between devices  54.7 us (27%)
  Pallas kernels  39 us (20%)
  local copies, waits for them, and re-layouts  10.7 us (5%)
    ppermute x11, waiting for transfers between devices, swap(): return lax.ppermute(value, axis, [(0, 1), (1, 0)])  27.1 us
    ppermute x6, waiting for transfers between devices, left(): return lax.ppermute(after(value, *others), 'x', ring(4, -1))  26.1 us
    ppermute x11, starting transfers between devices, swap(): return lax.ppermute(value, axis, [(0, 1), (1, 0)])  22.6 us
    pallas_call x2, Pallas kernels, project_part(): pl.pallas_call(functools.partial(project_kernel, steps, counts, bool(sums...  20.7 us
    ppermute x6, waiting for transfers between devices, right(): return lax.ppermute(after(value, *others), 'x', ring(4, 1))  15.9 us
    ppermute x2, waiting for transfers between devices, reduce_z(): from_below = lax.ppermute(up, 'z', ring(4, 1))  14 us
    ppermute x6, starting transfers between devices, left(): return lax.ppermute(after(value, *others), 'x', ring(4, -1))  12.4 us
    pallas_call x1, Pallas kernels, scan(): pl.pallas_call(scan_kernel, grid_spec=pltpu.PrefetchScalarGridSpec(num_sc...  9.83 us
  transfers between devices with their start and end apart: 32, of which 15 were waited for; matrix products, arithmetic and copies ran while one was open for 2% of the time, Pallas kernels for 13%

profile of v3, /device:TPU:1, one launch (start us, length us, event | category | flops | bytes accessed | tf_op | source)
XLA Modules:
  0.0 199.2 jit_solution(15314307265332300529)
XLA Ops:
  2.1 2.5 %deal.1 = bf16[512,1408]{1,0:T(8,128)(2,1)} custom-call(bf16[32,4096]{1,0:T(8,128)(2,1)} %groups_ref.1, bf16[32,8192]{1,0:T(8,128)(2,1)} %input_ref.1, bf16[32,8192]{1,0:T(8,128)(2,1)} %gate_ref.1, bf16[32,128]{1,0:T(8,128)(2,1)} %step_ref.1), custom_call_target="tpu_custom_call" | custom-call | tf_op jit(solution)/shard_map/deal/pallas_call | solution.py:70
  4.6 6.7 %all-to-all-start = ((bf16[16,32,1408]{2,1,0:T(8,128)(2,1)}), bf16[16,32,1408]{2,1,0:T(8,128)(2,1)S(1)}, u32[]{:S(2)}, u32[]{:S(2)}) async-start(bf16[16,32,1408]{2,1,0:T(8,128)(2,1)} %bitcast.69), calls=%async_computation | async-start | bytes 2883584 | tf_op jit(solution)/shard_map/all_to_all | solution.py:426
  14.1 12.0 %collective-permute-done.1.refs_2_ = bf16[1024,256]{1,0:T(8,128)(2,1)S(1)} collective-permute-done((bf16[1024,256]{1,0:T(8,128)(2,1)S(1)}, bf16[1024,256]{1,0:T(8,128)(2,1)S(1)}, u32[]{:S(2)}, u32[]{:S(2)}) %collective-permute-start.1) | collective-permute-done | bytes 524320 | tf_op jit(solution)/shard_map/ppermute | solution.py:40
  27.7 2.7 %collective-permute-start.4 = (bf16[512,256]{1,0:T(8,128)(2,1)}, bf16[512,256]{1,0:T(8,128)(2,1)}, u32[]{:S(2)}, u32[]{:S(2)}) collective-permute-start(bf16[512,256]{1,0:T(8,128)(2,1)} %slice.131), channel_id=1, source_target_pairs={{0,48},{16,0},{32,16},{48,32},{1,49},{17,1},{33,17},{49,33},{2,50}... | collective-permute-start | bytes 786440 | tf_op jit(solution)/shard_map/ppermute | solution.py:44
  31.9 2.5 %collective-permute-start.7 = (bf16[528,1280]{1,0:T(8,128)(2,1)S(1)}, bf16[528,1280]{1,0:T(8,128)(2,1)S(1)}, u32[]{:S(2)}, u32[]{:S(2)}) collective-permute-start(bf16[528,1280]{1,0:T(8,128)(2,1)S(1)} %assemble.1.refs_0_), channel_id=1, source_target_pairs={{0,48},{16,0},{32,16},{48,32},{1,49},{17,1},{33,17},{49,33},{2,50}... | collective-permute-start | bytes 4055048 | tf_op jit(solution)/shard_map/ppermute | solution.py:44
  35.3 2.6 %collective-permute-start.5 = (bf16[528,1280]{1,0:T(8,128)(2,1)S(1)}, bf16[528,1280]{1,0:T(8,128)(2,1)}, u32[]{:S(2)}, u32[]{:S(2)}) collective-permute-start(bf16[528,1280]{1,0:T(8,128)(2,1)S(1)} %assemble.1.refs_0_), channel_id=1, source_target_pairs={{0,64},{64,0},{1,65},{65,1},{2,66},{66,2},{3,67},{67,3},{4,68},{68... | collective-permute-start | bytes 4055048 | tf_op jit(solution)/shard_map/ppermute | solution.py:32
  37.9 26.1 %collective-permute-done.7.refs_1_ = bf16[528,1280]{1,0:T(8,128)(2,1)S(1)} collective-permute-done((bf16[528,1280]{1,0:T(8,128)(2,1)S(1)}, bf16[528,1280]{1,0:T(8,128)(2,1)S(1)}, u32[]{:S(2)}, u32[]{:S(2)}) %collective-permute-start.7) | collective-permute-done | bytes 1351712 | tf_op jit(solution)/shard_map/ppermute | solution.py:44
  70.1 2.6 %collective-permute-start.10 = (bf16[1024,256]{1,0:T(8,128)(2,1)S(1)}, bf16[1024,256]{1,0:T(8,128)(2,1)S(1)}, u32[]{:S(2)}, u32[]{:S(2)}) collective-permute-start(bf16[1024,256]{1,0:T(8,128)(2,1)S(1)} %copy-done.14), channel_id=1, source_target_pairs={{0,64},{64,0},{1,65},{65,1},{2,66},{66,2},{3,67},{67,3},{4,68},{68... | collective-permute-start | bytes 1572872 | tf_op jit(solution)/shard_map/ppermute | solution.py:32
  72.7 10.4 %collective-permute-done.10.refs_3_ = bf16[1024,256]{1,0:T(8,128)(2,1)S(1)} collective-permute-done((bf16[1024,256]{1,0:T(8,128)(2,1)S(1)}, bf16[1024,256]{1,0:T(8,128)(2,1)S(1)}, u32[]{:S(2)}, u32[]{:S(2)}) %collective-permute-start.10) | collective-permute-done | bytes 524320 | tf_op jit(solution)/shard_map/ppermute | solution.py:32
  92.1 12.8 %project.2 = (f32[512,1408]{1,0:T(8,128)}, f32[512,1408]{1,0:T(8,128)}) custom-call(s32[5]{0:T(128)S(1)} %stack.107.table, bf16[512,4096]{1,0:T(8,128)(2,1)} %own_hbm.3, bf16[512,4096]{1,0:T(8,128)(2,1)} %collective-permute-done.oth_hbm, bf16[528,1280]{1,0:T(8,128)(2,1)S(1)} %assemble.1.refs_0_, bf16[528,1280]{1,0:T(8,128)(2,1)S(1)} %copy-done.1, ...), custom_call_target="tpu_custom_call" | custom-call | flops 6710886400 | bytes 19660800 | tf_op jit(solution)/shard_map/project/pallas_call | solution.py:164
  104.9 9.4 %collective-permute-done.14.refs_3_ = bf16[272,1280]{1,0:T(8,128)(2,1)S(1)} collective-permute-done((bf16[272,1280]{1,0:T(8,128)(2,1)}, bf16[272,1280]{1,0:T(8,128)(2,1)S(1)}, u32[]{:S(2)}, u32[]{:S(2)}) %collective-permute-start.14) | collective-permute-done | bytes 696352 | tf_op jit(solution)/shard_map/ppermute | solution.py:32
  114.4 7.8 %project.3 = (bf16[512,1408]{1,0:T(8,128)(2,1)S(1)}, bf16[512,1408]{1,0:T(8,128)(2,1)}) custom-call(s32[3]{0:T(128)S(1)} %pad_add_fusion.1.table, bf16[512,4096]{1,0:T(8,128)(2,1)} %own_hbm.3, bf16[512,4096]{1,0:T(8,128)(2,1)} %collective-permute-done.oth_hbm, bf16[528,1280]{1,0:T(8,128)(2,1)S(1)} %collective-permute-done.11.refs_0_, ...), custom_call_target="tpu_custom_call" | custom-call | flops 4026531840 | bytes 14942208 | tf_op jit(solution)/shard_map/project/pallas_call | solution.py:164
  123.4 4.6 %collective-permute-start.15 = (bf16[512,1408]{1,0:T(8,128)(2,1)}, bf16[512,1408]{1,0:T(8,128)(2,1)S(1)}, u32[]{:S(2)}, u32[]{:S(2)}) collective-permute-start(bf16[512,1408]{1,0:T(8,128)(2,1)} %get-tuple-element.28), channel_id=1, source_target_pairs={{0,8},{8,0},{1,9},{9,1},{2,10},{10,2},{3,11},{11,3},{4,12},{12,4},... | collective-permute-start | bytes 4325384 | tf_op jit(solution)/shard_map/ppermute | solution.py:32
  130.6 2.7 %collective-permute-start.17 = (bf16[1024,256]{1,0:T(8,128)(2,1)}, bf16[1024,256]{1,0:T(8,128)(2,1)S(1)}, u32[]{:S(2)}, u32[]{:S(2)}) collective-permute-start(bf16[1024,256]{1,0:T(8,128)(2,1)} %copy-done.16), channel_id=1, source_target_pairs={{0,48},{16,0},{32,16},{48,32},{1,49},{17,1},{33,17},{49,33},{2,50}... | collective-permute-start | bytes 1572872 | tf_op jit(solution)/shard_map/ppermute | solution.py:44
  134.8 9.8 %scan.1 = (bf16[512,1024]{1,0:T(8,128)(2,1)S(1)}, f32[4,16,64,256]{3,2,1,0:T(8,128)}) custom-call(s32[13]{0:T(128)S(1)} %pad_add_fusion.info, bf16[512,1408]{1,0:T(8,128)(2,1)S(1)} %copy-done.11, bf16[512,1408]{1,0:T(8,128)(2,1)S(1)} %collective-permute-done.15.got, bf16[4,3,1024]{2,1,0:T(4,128)(2,1)S(1)} %copy.21.tail_x, ...), custom_call_target="tpu_custom_call" | custom-call | flops 2000000000 | bytes 14000000 | tf_op jit(solution)/shard_map/scan/pallas_call | solution.py:286
  148.7 4.5 %multiply.1 = (bf16[1024,1024]{1,0:T(8,128)(2,1)S(1)}, bf16[1024,1024]{1,0:T(8,128)(2,1)S(1)}) custom-call(bf16[512,1024]{1,0:T(8,128)(2,1)S(1)} %get-tuple-element.32.own_ref, bf16[512,1024]{1,0:T(8,128)(2,1)S(1)} %collective-permute-done.19.oth_ref, bf16[1024,256]{1,0:T(8,128)(2,1)S(1)} %copy-done.15, bf16[1024,256]{1,0:T(8,128)(2,1)S(1)} %copy-done.7, ...), custom_call_target="tpu_custom_call" | custom-call | flops 4294967296 | bytes 10485760 | tf_op jit(solution)/shard_map/multiply/pallas_call | solution.py:360
  156.3 5.8 %collective-permute-done.25 = bf16[256,512]{1,0:T(8,128)(2,1)S(1)} collective-permute-done((bf16[256,512]{1,0:T(8,128)(2,1)S(1)}, bf16[256,512]{1,0:T(8,128)(2,1)S(1)}, u32[]{:S(2)}, u32[]{:S(2)}) %collective-permute-start.25) | collective-permute-done | bytes 262176 | tf_op jit(solution)/shard_map/ppermute | solution.py:379
  162.5 2.7 %collective-permute-start.28 = (bf16[256,1024]{1,0:T(8,128)(2,1)S(1)}, bf16[256,1024]{1,0:T(8,128)(2,1)S(1)}, u32[]{:S(2)}, u32[]{:S(2)}) collective-permute-start(bf16[256,1024]{1,0:T(8,128)(2,1)S(1)} %pad_maximum_fusion.1), channel_id=1, source_target_pairs={{0,3},{1,0},{2,1},{3,2},{4,7},{5,4},{6,5},{7,6},{8,11},{9,8},{10,9... | collective-permute-start | bytes 1572872 | tf_op jit(solution)/shard_map/ppermute | solution.py:385
  165.2 10.6 %collective-permute-done.26 = bf16[256,1024]{1,0:T(8,128)(2,1)S(1)} collective-permute-done((bf16[256,1024]{1,0:T(8,128)(2,1)S(1)}, bf16[256,1024]{1,0:T(8,128)(2,1)S(1)}, u32[]{:S(2)}, u32[]{:S(2)}) %collective-permute-start.26) | collective-permute-done | bytes 524320 | tf_op jit(solution)/shard_map/ppermute | solution.py:384
  176.1 3.9 %collective-permute-done.20 = bf16[8,64,1024]{2,1,0:T(8,128)(2,1)S(1)} collective-permute-done((bf16[8,64,1024]{2,1,0:T(8,128)(2,1)S(1)}, bf16[8,64,1024]{2,1,0:T(8,128)(2,1)S(1)}, u32[]{:S(2)}, u32[]{:S(2)}) %collective-permute-start.20) | collective-permute-done | bytes 1048608 | tf_op jit(solution)/shard_map/ppermute | solution.py:32
  180.9 2.7 %collective-permute-start.23 = (bf16[128,512]{1,0:T(8,128)(2,1)S(1)}, bf16[128,512]{1,0:T(8,128)(2,1)S(1)}, u32[]{:S(2)}, u32[]{:S(2)}) collective-permute-start(bf16[128,512]{1,0:T(8,128)(2,1)S(1)} %get-tuple-element.49), channel_id=1, source_target_pairs={{0,3},{1,0},{2,1},{3,2},{4,7},{5,4},{6,5},{7,6},{8,11},{9,8},{10,9... | collective-permute-start | bytes 393224 | tf_op jit(solution)/shard_map/ppermute | solution.py:380
  185.8 2.9 %collective-permute-start.24 = (bf16[128,1024]{1,0:T(8,128)(2,1)S(1)}, bf16[128,1024]{1,0:T(8,128)(2,1)S(1)}, u32[]{:S(2)}, u32[]{:S(2)}) collective-permute-start(bf16[128,1024]{1,0:T(8,128)(2,1)S(1)} %pad_maximum_fusion.4), channel_id=1, source_target_pairs={{0,3},{1,0},{2,1},{3,2},{4,7},{5,4},{6,5},{7,6},{8,11},{9,8},{10,9... | collective-permute-start | bytes 786440 | tf_op jit(solution)/shard_map/ppermute | solution.py:385
  188.8 3.4 %collective-permute-done.22 = bf16[128,1024]{1,0:T(8,128)(2,1)S(1)} collective-permute-done((bf16[128,1024]{1,0:T(8,128)(2,1)S(1)}, bf16[128,1024]{1,0:T(8,128)(2,1)S(1)}, u32[]{:S(2)}, u32[]{:S(2)}) %collective-permute-start.22) | collective-permute-done | bytes 262176 | tf_op jit(solution)/shard_map/ppermute | solution.py:384
  192.4 4.3 %collective-permute-start.30 = (bf16[64,2048]{1,0:T(8,128)(2,1)S(1)}, bf16[64,2048]{1,0:T(8,128)(2,1)S(1)}, u32[]{:S(2)}, u32[]{:S(2)}) collective-permute-start(bf16[64,2048]{1,0:T(8,128)(2,1)S(1)} %get-tuple-element.46), channel_id=1, source_target_pairs={{0,8},{8,0},{1,9},{9,1},{2,10},{10,2},{3,11},{11,3},{4,12},{12,4},... | collective-permute-start | bytes 786440 | tf_op jit(solution)/shard_map/ppermute | solution.py:32
  (136 shorter events, 42.0 us)
Async XLA Ops:
  0.6 87.7 %collective-permute-start = (bf16[512,4096]{1,0:T(8,128)(2,1)}, bf16[512,4096]{1,0:T(8,128)(2,1)}, u32[]{:S(2)}, u32[]{:S(2)}) collective-permute-start(bf16[512,4096]{1,0:T(8,128)(2,1)} %own_hbm.3), channel_id=1, source_target_pairs={{0,8},{8,0},{1,9},{9,1},{2,10},{10,2},{3,11},{11,3},{4,12},{12,4},... | collective-permute-start | bytes 12582920 | tf_op jit(solution)/shard_map/ppermute | solution.py:32
  4.6 27.2 %all-to-all-start = ((bf16[16,32,1408]{2,1,0:T(8,128)(2,1)}), bf16[16,32,1408]{2,1,0:T(8,128)(2,1)S(1)}, u32[]{:S(2)}, u32[]{:S(2)}) async-start(bf16[16,32,1408]{2,1,0:T(8,128)(2,1)} %bitcast.69), calls=%async_computation | async-start | bytes 2883584 | tf_op jit(solution)/shard_map/all_to_all | solution.py:426
  11.3 14.8 %collective-permute-start.1 = (bf16[1024,256]{1,0:T(8,128)(2,1)S(1)}, bf16[1024,256]{1,0:T(8,128)(2,1)S(1)}, u32[]{:S(2)}, u32[]{:S(2)}) collective-permute-start(bf16[1024,256]{1,0:T(8,128)(2,1)S(1)} %copy-done.14), channel_id=1, source_target_pairs={{0,16},{16,32},{32,48},{48,0},{1,17},{17,33},{33,49},{49,1},{2,18}... | collective-permute-start | bytes 1572872 | tf_op jit(solution)/shard_map/ppermute | solution.py:40
  12.6 14.2 %collective-permute-start.3 = (bf16[1024,256]{1,0:T(8,128)(2,1)S(1)}, bf16[1024,256]{1,0:T(8,128)(2,1)S(1)}, u32[]{:S(2)}, u32[]{:S(2)}) collective-permute-start(bf16[1024,256]{1,0:T(8,128)(2,1)S(1)} %copy-done.14), channel_id=1, source_target_pairs={{0,48},{16,0},{32,16},{48,32},{1,49},{17,1},{33,17},{49,33},{2,50}... | collective-permute-start | bytes 1572872 | tf_op jit(solution)/shard_map/ppermute | solution.py:44
  26.8 8.5 %collective-permute-start.2 = (bf16[512,256]{1,0:T(8,128)(2,1)}, bf16[512,256]{1,0:T(8,128)(2,1)}, u32[]{:S(2)}, u32[]{:S(2)}) collective-permute-start(bf16[512,256]{1,0:T(8,128)(2,1)} %slice.130), channel_id=1, source_target_pairs={{0,16},{16,32},{32,48},{48,0},{1,17},{17,33},{33,49},{49,1},{2,18}... | collective-permute-start | bytes 786440 | tf_op jit(solution)/shard_map/ppermute | solution.py:40
  31.9 32.1 %collective-permute-start.7 = (bf16[528,1280]{1,0:T(8,128)(2,1)S(1)}, bf16[528,1280]{1,0:T(8,128)(2,1)S(1)}, u32[]{:S(2)}, u32[]{:S(2)}) collective-permute-start(bf16[528,1280]{1,0:T(8,128)(2,1)S(1)} %assemble.1.refs_0_), channel_id=1, source_target_pairs={{0,48},{16,0},{32,16},{48,32},{1,49},{17,1},{33,17},{49,33},{2,50}... | collective-permute-start | bytes 4055048 | tf_op jit(solution)/shard_map/ppermute | solution.py:44
  34.5 32.0 %collective-permute-start.6 = (bf16[528,1280]{1,0:T(8,128)(2,1)S(1)}, bf16[528,1280]{1,0:T(8,128)(2,1)S(1)}, u32[]{:S(2)}, u32[]{:S(2)}) collective-permute-start(bf16[528,1280]{1,0:T(8,128)(2,1)S(1)} %assemble.1.refs_0_), channel_id=1, source_target_pairs={{0,16},{16,32},{32,48},{48,0},{1,17},{17,33},{33,49},{49,1},{2,18}... | collective-permute-start | bytes 4055048 | tf_op jit(solution)/shard_map/ppermute | solution.py:40
  35.3 34.7 %collective-permute-start.5 = (bf16[528,1280]{1,0:T(8,128)(2,1)S(1)}, bf16[528,1280]{1,0:T(8,128)(2,1)}, u32[]{:S(2)}, u32[]{:S(2)}) collective-permute-start(bf16[528,1280]{1,0:T(8,128)(2,1)S(1)} %assemble.1.refs_0_), channel_id=1, source_target_pairs={{0,64},{64,0},{1,65},{65,1},{2,66},{66,2},{3,67},{67,3},{4,68},{68... | collective-permute-start | bytes 4055048 | tf_op jit(solution)/shard_map/ppermute | solution.py:32
  66.5 16.6 %collective-permute-start.9 = (bf16[272,1280]{1,0:T(8,128)(2,1)S(1)}, bf16[272,1280]{1,0:T(8,128)(2,1)S(1)}, u32[]{:S(2)}, u32[]{:S(2)}) collective-permute-start(bf16[272,1280]{1,0:T(8,128)(2,1)S(1)} %slice.133), channel_id=1, source_target_pairs={{0,48},{16,0},{32,16},{48,32},{1,49},{17,1},{33,17},{49,33},{2,50}... | collective-permute-start | bytes 2088968 | tf_op jit(solution)/shard_map/ppermute | solution.py:44
  67.7 15.4 %collective-permute-start.8 = (bf16[256,1280]{1,0:T(8,128)(2,1)S(1)}, bf16[256,1280]{1,0:T(8,128)(2,1)}, u32[]{:S(2)}, u32[]{:S(2)}) collective-permute-start(bf16[256,1280]{1,0:T(8,128)(2,1)S(1)} %slice.132), channel_id=1, source_target_pairs={{0,16},{16,32},{32,48},{48,0},{1,17},{17,33},{33,49},{49,1},{2,18}... | collective-permute-start | bytes 1966088 | tf_op jit(solution)/shard_map/ppermute | solution.py:40
  70.1 13.0 %collective-permute-start.10 = (bf16[1024,256]{1,0:T(8,128)(2,1)S(1)}, bf16[1024,256]{1,0:T(8,128)(2,1)S(1)}, u32[]{:S(2)}, u32[]{:S(2)}) collective-permute-start(bf16[1024,256]{1,0:T(8,128)(2,1)S(1)} %copy-done.14), channel_id=1, source_target_pairs={{0,64},{64,0},{1,65},{65,1},{2,66},{66,2},{3,67},{67,3},{4,68},{68... | collective-permute-start | bytes 1572872 | tf_op jit(solution)/shard_map/ppermute | solution.py:32
  83.1 31.2 %collective-permute-start.11 = (bf16[528,1280]{1,0:T(8,128)(2,1)}, bf16[528,1280]{1,0:T(8,128)(2,1)S(1)}, u32[]{:S(2)}, u32[]{:S(2)}) collective-permute-start(bf16[528,1280]{1,0:T(8,128)(2,1)} %collective-permute-done.5.refs_3_), channel_id=1, source_target_pairs={{0,48},{16,0},{32,16},{48,32},{1,49},{17,1},{33,17},{49,33},{2,50}... | collective-permute-start | bytes 4055048 | tf_op jit(solution)/shard_map/ppermute | solution.py:44
  85.0 29.3 %collective-permute-start.12 = (bf16[528,1280]{1,0:T(8,128)(2,1)}, bf16[528,1280]{1,0:T(8,128)(2,1)}, u32[]{:S(2)}, u32[]{:S(2)}) collective-permute-start(bf16[528,1280]{1,0:T(8,128)(2,1)} %collective-permute-done.5.refs_3_), channel_id=1, source_target_pairs={{0,16},{16,32},{32,48},{48,0},{1,17},{17,33},{33,49},{49,1},{2,18}... | collective-permute-start | bytes 4055048 | tf_op jit(solution)/shard_map/ppermute | solution.py:40
  85.1 19.8 %collective-permute-start.13 = (bf16[256,1280]{1,0:T(8,128)(2,1)}, bf16[256,1280]{1,0:T(8,128)(2,1)}, u32[]{:S(2)}, u32[]{:S(2)}) collective-permute-start(bf16[256,1280]{1,0:T(8,128)(2,1)} %collective-permute-done.8.refs_4_), channel_id=1, source_target_pairs={{0,64},{64,0},{1,65},{65,1},{2,66},{66,2},{3,67},{67,3},{4,68},{68... | collective-permute-start | bytes 1966088 | tf_op jit(solution)/shard_map/ppermute | solution.py:32
  87.6 26.7 %collective-permute-start.14 = (bf16[272,1280]{1,0:T(8,128)(2,1)}, bf16[272,1280]{1,0:T(8,128)(2,1)S(1)}, u32[]{:S(2)}, u32[]{:S(2)}) collective-permute-start(bf16[272,1280]{1,0:T(8,128)(2,1)} %copy-done.12), channel_id=1, source_target_pairs={{0,64},{64,0},{1,65},{65,1},{2,66},{66,2},{3,67},{67,3},{4,68},{68... | collective-permute-start | bytes 2088968 | tf_op jit(solution)/shard_map/ppermute | solution.py:32
  123.4 10.1 %collective-permute-start.15 = (bf16[512,1408]{1,0:T(8,128)(2,1)}, bf16[512,1408]{1,0:T(8,128)(2,1)S(1)}, u32[]{:S(2)}, u32[]{:S(2)}) collective-permute-start(bf16[512,1408]{1,0:T(8,128)(2,1)} %get-tuple-element.28), channel_id=1, source_target_pairs={{0,8},{8,0},{1,9},{9,1},{2,10},{10,2},{3,11},{11,3},{4,12},{12,4},... | collective-permute-start | bytes 4325384 | tf_op jit(solution)/shard_map/ppermute | solution.py:32
  128.2 16.5 %collective-permute-start.18 = (bf16[1024,256]{1,0:T(8,128)(2,1)S(1)}, bf16[1024,256]{1,0:T(8,128)(2,1)S(1)}, u32[]{:S(2)}, u32[]{:S(2)}) collective-permute-start(bf16[1024,256]{1,0:T(8,128)(2,1)S(1)} %copy-done.9), channel_id=1, source_target_pairs={{0,64},{64,0},{1,65},{65,1},{2,66},{66,2},{3,67},{67,3},{4,68},{68... | collective-permute-start | bytes 1572872 | tf_op jit(solution)/shard_map/ppermute | solution.py:32
  130.6 14.7 %collective-permute-start.16 = (bf16[1024,256]{1,0:T(8,128)(2,1)}, bf16[1024,256]{1,0:T(8,128)(2,1)S(1)}, u32[]{:S(2)}, u32[]{:S(2)}) collective-permute-start(bf16[1024,256]{1,0:T(8,128)(2,1)} %copy-done.16), channel_id=1, source_target_pairs={{0,16},{16,32},{32,48},{48,0},{1,17},{17,33},{33,49},{49,1},{2,18}... | collective-permute-start | bytes 1572872 | tf_op jit(solution)/shard_map/ppermute | solution.py:40
  130.6 14.7 %collective-permute-start.17 = (bf16[1024,256]{1,0:T(8,128)(2,1)}, bf16[1024,256]{1,0:T(8,128)(2,1)S(1)}, u32[]{:S(2)}, u32[]{:S(2)}) collective-permute-start(bf16[1024,256]{1,0:T(8,128)(2,1)} %copy-done.16), channel_id=1, source_target_pairs={{0,48},{16,0},{32,16},{48,32},{1,49},{17,1},{33,17},{49,33},{2,50}... | collective-permute-start | bytes 1572872 | tf_op jit(solution)/shard_map/ppermute | solution.py:44
  153.3 8.8 %collective-permute-start.25 = (bf16[256,512]{1,0:T(8,128)(2,1)S(1)}, bf16[256,512]{1,0:T(8,128)(2,1)S(1)}, u32[]{:S(2)}, u32[]{:S(2)}) collective-permute-start(bf16[256,512]{1,0:T(8,128)(2,1)S(1)} %get-tuple-element.38), channel_id=1, source_target_pairs={{0,1},{1,2},{2,3},{3,0},{4,5},{5,6},{6,7},{7,4},{8,9},{9,10},{10,1... | collective-permute-start | bytes 786440 | tf_op jit(solution)/shard_map/ppermute | solution.py:379
  153.8 8.3 %collective-permute-start.27 = (bf16[256,512]{1,0:T(8,128)(2,1)S(1)}, bf16[256,512]{1,0:T(8,128)(2,1)S(1)}, u32[]{:S(2)}, u32[]{:S(2)}) collective-permute-start(bf16[256,512]{1,0:T(8,128)(2,1)S(1)} %get-tuple-element.39), channel_id=1, source_target_pairs={{0,3},{1,0},{2,1},{3,2},{4,7},{5,4},{6,5},{7,6},{8,11},{9,8},{10,9... | collective-permute-start | bytes 786440 | tf_op jit(solution)/shard_map/ppermute | solution.py:380
  156.2 23.8 %collective-permute-start.20 = (bf16[8,64,1024]{2,1,0:T(8,128)(2,1)S(1)}, bf16[8,64,1024]{2,1,0:T(8,128)(2,1)S(1)}, u32[]{:S(2)}, u32[]{:S(2)}) collective-permute-start(bf16[8,64,1024]{2,1,0:T(8,128)(2,1)S(1)} %slice_bitcast_fusion), channel_id=1, source_target_pairs={{0,4},{4,0},{1,5},{5,1},{2,6},{6,2},{3,7},{7,3},{8,12},{12,8},{9,1... | collective-permute-start | bytes 3145736 | tf_op jit(solution)/shard_map/ppermute | solution.py:32
  162.3 13.5 %collective-permute-start.26 = (bf16[256,1024]{1,0:T(8,128)(2,1)S(1)}, bf16[256,1024]{1,0:T(8,128)(2,1)S(1)}, u32[]{:S(2)}, u32[]{:S(2)}) collective-permute-start(bf16[256,1024]{1,0:T(8,128)(2,1)S(1)} %pad_maximum_fusion), channel_id=1, source_target_pairs={{0,1},{1,2},{2,3},{3,0},{4,5},{5,6},{6,7},{7,4},{8,9},{9,10},{10,1... | collective-permute-start | bytes 1572872 | tf_op jit(solution)/shard_map/ppermute | solution.py:384
  162.5 13.3 %collective-permute-start.28 = (bf16[256,1024]{1,0:T(8,128)(2,1)S(1)}, bf16[256,1024]{1,0:T(8,128)(2,1)S(1)}, u32[]{:S(2)}, u32[]{:S(2)}) collective-permute-start(bf16[256,1024]{1,0:T(8,128)(2,1)S(1)} %pad_maximum_fusion.1), channel_id=1, source_target_pairs={{0,3},{1,0},{2,1},{3,2},{4,7},{5,4},{6,5},{7,6},{8,11},{9,8},{10,9... | collective-permute-start | bytes 1572872 | tf_op jit(solution)/shard_map/ppermute | solution.py:385
  (35 other events, 342.0 us)
